TPU v7x, 32 devices: a whole 2x2x4 slice. The times are simulated.
32 devices in a mesh: fsdp: 2 (over y), seq: 16 (over z, x, core).
Axes of the slice: x: 2, y: 2, z: 4, core: 2. Of those that a mesh axis runs over, the one named last changes fastest.
Arguments:
- inputs: bfloat16 [8, 1024, 1024], P('fsdp', 'seq'), may hold values from -6 to 6
- mixer_gain: bfloat16 [1024], P('fsdp'), may hold values from 0.5 to 1.5
- query_weight: bfloat16 [1024, 512], P('fsdp'), may hold values from -0.1875 to 0.1875
- key_weight: bfloat16 [1024, 512], P('fsdp'), may hold values from -0.1875 to 0.1875
- value_weight: bfloat16 [1024, 1024], P('fsdp'), may hold values from -0.1875 to 0.1875
- decay_down: bfloat16 [1024, 16], P('fsdp'), may hold values from -0.1875 to 0.1875
- decay_up: bfloat16 [16, 512], P('fsdp'), may hold values from -1.5 to 1.5
- decay_bias: bfloat16 [512], P('fsdp'), may hold values from -1 to 5
- outgate_weight: bfloat16 [1024, 1024], P('fsdp'), may hold values from -0.1875 to 0.1875
- head_gain: bfloat16 [256], P('fsdp'), may hold values from 0.5 to 1.5
- output_weight: bfloat16 [1024, 1024], P('fsdp'), may hold values from -0.1875 to 0.1875
- feed_gain: bfloat16 [1024], P('fsdp'), may hold values from 0.5 to 1.5
- feed_gate: bfloat16 [1024, 2816], P('fsdp'), may hold values from -0.1875 to 0.1875
- feed_up: bfloat16 [1024, 2816], P('fsdp'), may hold values from -0.1875 to 0.1875
- feed_down: bfloat16 [2816, 1024], P('fsdp'), may hold values from -0.109375 to 0.109375
- cotangent: bfloat16 [8, 1024, 1024], P('fsdp', 'seq'), may hold values from -6 to 6
Outputs:
- output: bfloat16 [8, 1024, 1024], P('fsdp', 'seq')
- input_grad: float32 [8, 1024, 1024], P('fsdp', 'seq')
- grad_mixer_gain: float32 [1024], P('fsdp')
- grad_query_weight: float32 [1024, 512], P('fsdp')
- grad_key_weight: float32 [1024, 512], P('fsdp')
- grad_value_weight: float32 [1024, 1024], P('fsdp')
- grad_decay_down: float32 [1024, 16], P('fsdp')
- grad_decay_up: float32 [16, 512], P('fsdp')
- grad_decay_bias: float32 [512], P('fsdp')
- grad_outgate_weight: float32 [1024, 1024], P('fsdp')
- grad_head_gain: float32 [256], P('fsdp')
- grad_output_weight: float32 [1024, 1024], P('fsdp')
- grad_feed_gain: float32 [1024], P('fsdp')
- grad_feed_gate: float32 [1024, 2816], P('fsdp')
- grad_feed_up: float32 [1024, 2816], P('fsdp')
- grad_feed_down: float32 [2816, 1024], P('fsdp')
All inputs are finite; a program needn't handle non-finite values.
Results may differ from a plain program's by a relative error of at most 0.014.
Values may be sent and summed in bfloat16 or wider, within the bound.
No kernel may reach another device: no remote copies, remote signals or barrier semaphores. Data moves between devices by JAX's collectives and lax.ppermute only.
A program may use at most 320 MiB of HBM per device.

v0:
```python
import jax
import jax.numpy as jnp
from jax import lax
from jax.sharding import PartitionSpec as P

H = 4
DK = 128
DV = 256
SPAN = 64


epsilon = 1e-06
head_floor = 0.25
gate_scale = 16.0
highest = lax.Precision.HIGHEST


def rms_scale(values, scale_gain):
    return (
        values * lax.rsqrt(jnp.mean(values * values, axis=-1, keepdims=True) + epsilon) * scale_gain
    )


def head_scale(values, scale_gain):
    return (
        values
        * lax.rsqrt(jnp.maximum(jnp.mean(values * values, axis=-1, keepdims=True), head_floor))
        * scale_gain
    )


def swiglu(gate_part, up_part):
    return jax.nn.silu(gate_part) * up_part


def head_mix(mixed, out_gate, head_gain):
    row_count = mixed.shape[0]
    normed = head_scale(mixed, head_gain)
    return (normed * jax.nn.silu(out_gate.reshape(mixed.shape))).reshape(row_count, -1)


def span_mix(query, keys, decay, values):
    length, key_width = query.shape
    blocks = length // SPAN
    shaped_q = query.reshape(blocks, SPAN, key_width) * key_width ** (-0.5)
    shaped_k = keys.reshape(blocks, SPAN, key_width)
    shaped_v = values.reshape(blocks, SPAN, values.shape[1])
    cumulative = jnp.cumsum(decay.reshape(blocks, SPAN, key_width), axis=1)
    span_end = cumulative[:, SPAN - 1 :, :]
    q_tilde = shaped_q * jnp.exp(cumulative)
    k_tilde = shaped_k * jnp.exp(-cumulative)
    k_tail = shaped_k * jnp.exp(span_end - cumulative)
    scores = jnp.einsum("bik,bjk->bij", q_tilde, k_tilde, precision=highest)
    row_index = lax.broadcasted_iota(jnp.int32, (SPAN, SPAN), 0)
    col_index = lax.broadcasted_iota(jnp.int32, (SPAN, SPAN), 1)
    scores = jnp.where(row_index >= col_index, scores, 0.0)
    inside = jnp.einsum("bij,bjv->biv", scores, shaped_v, precision=highest)
    updates = jnp.einsum("bjk,bjv->bkv", k_tail, shaped_v, precision=highest)
    span_fade = jnp.exp(span_end[:, 0, :])

    def advance(carried, pieces):
        fade_rate, update = pieces
        return (carried * fade_rate[:, None] + update, carried)

    initial = jnp.zeros((key_width, values.shape[1]), jnp.float32)
    _, before = lax.scan(advance, initial, (span_fade, updates))
    outside = jnp.einsum("bik,bkv->biv", q_tilde, before, precision=highest)
    return (inside + outside).reshape(length, values.shape[1])


def mat_product(left, right):
    return jnp.dot(left, right, preferred_element_type=jnp.float32)


def cross_rows(left, right):
    return lax.dot_general(
        left, right, (((0,), (0,)), ((), ())), preferred_element_type=jnp.float32
    )


def back_product(left, right):
    return lax.dot_general(
        left, right, (((1,), (1,)), ((), ())), preferred_element_type=jnp.float32
    )


def per_device(
    inputs,
    mixer_gain,
    query_weight,
    key_weight,
    value_weight,
    decay_down,
    decay_up,
    decay_bias,
    outgate_weight,
    head_gain,
    output_weight,
    feed_gain,
    feed_gate,
    feed_up,
    feed_down,
    cotangent,
):
    gathered = (
        lax.all_gather(mixer_gain, "fsdp", axis=0, tiled=True),
        lax.all_gather(query_weight, "fsdp", axis=0, tiled=True),
        lax.all_gather(key_weight, "fsdp", axis=0, tiled=True),
        lax.all_gather(value_weight, "fsdp", axis=0, tiled=True),
        lax.all_gather(decay_down, "fsdp", axis=0, tiled=True),
        lax.all_gather(decay_up, "fsdp", axis=0, tiled=True),
        lax.all_gather(decay_bias, "fsdp", axis=0, tiled=True),
        lax.all_gather(outgate_weight, "fsdp", axis=0, tiled=True),
        lax.all_gather(head_gain, "fsdp", axis=0, tiled=True),
        lax.all_gather(output_weight, "fsdp", axis=0, tiled=True),
        lax.all_gather(feed_gain, "fsdp", axis=0, tiled=True),
        lax.all_gather(feed_gate, "fsdp", axis=0, tiled=True),
        lax.all_gather(feed_up, "fsdp", axis=0, tiled=True),
        lax.all_gather(feed_down, "fsdp", axis=0, tiled=True),
    )
    (
        full_mixer_gain,
        full_query,
        full_key,
        full_value,
        full_down,
        full_up_rank,
        full_bias,
        full_outgate,
        full_head_gain,
        full_output,
        full_feed_gain,
        full_feed_gate,
        full_feed_up,
        full_feed_down,
    ) = gathered
    seq_count, seg_rows, model_width = inputs.shape
    row_count = seq_count * seg_rows
    seq_devices = lax.axis_size("seq")
    groups = seq_devices // (seq_count * H)
    col_count = DV // groups
    residual_in = inputs.reshape(row_count, model_width).astype(jnp.float32)
    normed_full, first_pull = jax.vjp(rms_scale, residual_in, full_mixer_gain.astype(jnp.float32))
    normed = normed_full.astype(jnp.bfloat16)
    query = mat_product(normed, full_query).astype(jnp.bfloat16)
    keys = mat_product(normed, full_key).astype(jnp.bfloat16)
    values = mat_product(normed, full_value).astype(jnp.bfloat16)
    ranked = mat_product(normed, full_down).astype(jnp.bfloat16)
    decay_in = mat_product(ranked, full_up_rank) + full_bias.astype(jnp.float32)
    decay = (jax.nn.log_sigmoid(decay_in) / gate_scale).astype(jnp.bfloat16)
    out_gate = mat_product(normed, full_outgate)

    def head_rows(array):
        return array.reshape(seq_count, seg_rows, H, DK)

    stacked = jnp.concatenate((head_rows(query), head_rows(keys), head_rows(decay)), axis=3)
    stacked = stacked.transpose(0, 2, 1, 3)
    stacked = jnp.broadcast_to(stacked[:, :, None], (seq_count, H, groups, seg_rows, 3 * DK))
    stacked = stacked.reshape(seq_devices * seg_rows, 3 * DK)
    value_send = values.reshape(seq_count, seg_rows, H, groups, col_count).transpose(0, 2, 3, 1, 4)
    value_send = value_send.reshape(seq_devices * seg_rows, col_count)
    head_qkd, head_values = (
        lax.all_to_all(stacked, "seq", split_axis=0, concat_axis=0, tiled=True),
        lax.all_to_all(value_send, "seq", split_axis=0, concat_axis=0, tiled=True),
    )
    mixed_local, mix_pull = jax.vjp(
        span_mix,
        head_qkd[:, :DK].astype(jnp.float32),
        head_qkd[:, DK : 2 * DK].astype(jnp.float32),
        head_qkd[:, 2 * DK :].astype(jnp.float32),
        head_values.astype(jnp.float32),
    )
    returned = lax.all_to_all(
        mixed_local.astype(jnp.bfloat16), "seq", split_axis=0, concat_axis=0, tiled=True
    )
    mixed_rows = returned.reshape(seq_count, H, groups, seg_rows, col_count).transpose(
        0, 3, 1, 2, 4
    )
    mixed_rows = mixed_rows.reshape(row_count, H, DV).astype(jnp.float32)
    gated_full, head_pull = jax.vjp(
        head_mix, mixed_rows, out_gate, full_head_gain.astype(jnp.float32)
    )
    gated = gated_full.astype(jnp.bfloat16)
    middle = residual_in + mat_product(gated, full_output)
    second_full, second_pull = jax.vjp(rms_scale, middle, full_feed_gain.astype(jnp.float32))
    second_norm = second_full.astype(jnp.bfloat16)
    gate_part = mat_product(second_norm, full_feed_gate)
    up_part = mat_product(second_norm, full_feed_up)
    hidden_full, act_pull = jax.vjp(swiglu, gate_part, up_part)
    hidden = hidden_full.astype(jnp.bfloat16)
    final = middle + mat_product(hidden, full_feed_down)
    output = final.astype(jnp.bfloat16).reshape(seq_count, seg_rows, model_width)
    seq_grad = cotangent.reshape(row_count, model_width).astype(jnp.float32)
    d_down = seq_grad.astype(jnp.bfloat16)
    grad_feed_down = cross_rows(hidden, d_down)
    d_hidden = back_product(d_down, full_feed_down)
    d_gate_full, d_up_full = act_pull(d_hidden)
    d_gate = d_gate_full.astype(jnp.bfloat16)
    d_up = d_up_full.astype(jnp.bfloat16)
    grad_feed_gate = cross_rows(second_norm, d_gate)
    grad_feed_up = cross_rows(second_norm, d_up)
    d_second = back_product(d_gate, full_feed_gate) + back_product(d_up, full_feed_up)
    d_middle_norm, grad_feed_gain = second_pull(d_second)
    d_middle = seq_grad + d_middle_norm
    d_branch = d_middle.astype(jnp.bfloat16)
    grad_output_weight = cross_rows(gated, d_branch)
    d_gated = back_product(d_branch, full_output)
    d_mixed, d_outgate_full, grad_head_gain = head_pull(d_gated)
    d_mixed_low = d_mixed.astype(jnp.bfloat16)
    mixed_send = d_mixed_low.reshape(seq_count, seg_rows, H, groups, col_count).transpose(
        0, 2, 3, 1, 4
    )
    mixed_send = mixed_send.reshape(seq_devices * seg_rows, col_count)
    head_grad = lax.all_to_all(mixed_send, "seq", split_axis=0, concat_axis=0, tiled=True)
    d_query_part, d_keys_part, d_decay_part, d_values_part = mix_pull(head_grad.astype(jnp.float32))
    back_qkd, back_values = (
        lax.all_to_all(
            jnp.concatenate((d_query_part, d_keys_part, d_decay_part), axis=1).astype(jnp.bfloat16),
            "seq",
            split_axis=0,
            concat_axis=0,
            tiled=True,
        ).astype(jnp.float32),
        lax.all_to_all(
            d_values_part.astype(jnp.bfloat16), "seq", split_axis=0, concat_axis=0, tiled=True
        ).astype(d_values_part.dtype),
    )
    summed = (
        back_qkd.reshape(seq_count, H, groups, seg_rows, 3 * DK).sum(axis=2).transpose(0, 2, 1, 3)
    )
    d_query = summed[..., :DK].reshape(row_count, H * DK).astype(jnp.bfloat16)
    d_keys = summed[..., DK : 2 * DK].reshape(row_count, H * DK).astype(jnp.bfloat16)
    d_decay = summed[..., 2 * DK :].reshape(row_count, H * DK).astype(jnp.bfloat16)
    d_values = back_values.reshape(seq_count, H, groups, seg_rows, col_count).transpose(
        0, 3, 1, 2, 4
    )
    d_values = d_values.reshape(row_count, H * DV).astype(jnp.bfloat16)
    d_decay_in = d_decay.astype(jnp.float32) * jax.nn.sigmoid(-decay_in) / gate_scale
    grad_decay_bias = jnp.sum(d_decay_in, axis=0)
    grad_decay_up = lax.dot_general(
        ranked.astype(jnp.float32), d_decay_in, (((0,), (0,)), ((), ())), precision=highest
    )
    d_ranked = lax.dot_general(
        d_decay_in, full_up_rank.astype(jnp.float32), (((1,), (1,)), ((), ())), precision=highest
    ).astype(jnp.bfloat16)
    d_outgate = d_outgate_full.astype(jnp.bfloat16)
    grad_query_weight = cross_rows(normed, d_query)
    grad_key_weight = cross_rows(normed, d_keys)
    grad_value_weight = cross_rows(normed, d_values)
    grad_outgate_weight = cross_rows(normed, d_outgate)
    grad_decay_down = cross_rows(normed, d_ranked)
    d_normed = (
        back_product(d_query, full_query)
        + back_product(d_keys, full_key)
        + back_product(d_values, full_value)
        + back_product(d_outgate, full_outgate)
        + back_product(d_ranked, full_down)
    )
    d_input_norm, grad_mixer_gain = first_pull(d_normed)
    input_grad = (d_middle + d_input_norm).reshape(seq_count, seg_rows, model_width)
    gradients = (
        grad_mixer_gain,
        grad_query_weight,
        grad_key_weight,
        grad_value_weight,
        grad_decay_down,
        grad_decay_up,
        grad_decay_bias,
        grad_outgate_weight,
        grad_head_gain,
        grad_output_weight,
        grad_feed_gain,
        grad_feed_gate,
        grad_feed_up,
        grad_feed_down,
    )
    fsdp_count = lax.axis_size("fsdp")
    packed = jnp.concatenate([gradient.reshape(fsdp_count, -1) for gradient in gradients], axis=1)
    shard_sum = lax.psum_scatter(
        packed.reshape(-1), ("fsdp", "seq"), scatter_dimension=0, tiled=True
    )
    own_half = lax.all_gather(shard_sum.astype(jnp.bfloat16), "seq", axis=0, tiled=True).astype(
        shard_sum.dtype
    )
    results = []
    offset = 0
    for gradient in gradients:
        piece_size = gradient.size // fsdp_count
        results.append(
            own_half[offset : offset + piece_size].reshape(
                (gradient.shape[0] // fsdp_count,) + gradient.shape[1:]
            )
        )
        offset += piece_size
    return (output, input_grad) + tuple(results)


def solution(mesh):
    return jax.shard_map(
        per_device,
        mesh=mesh,
        in_specs=(
            P("fsdp", "seq", None),
            P("fsdp"),
            P("fsdp", None),
            P("fsdp", None),
            P("fsdp", None),
            P("fsdp", None),
            P("fsdp", None),
            P("fsdp"),
            P("fsdp", None),
            P("fsdp"),
            P("fsdp", None),
            P("fsdp"),
            P("fsdp", None),
            P("fsdp", None),
            P("fsdp", None),
            P("fsdp", "seq", None),
        ),
        out_specs=(
            P("fsdp", "seq", None),
            P("fsdp", "seq", None),
            P("fsdp"),
            P("fsdp", None),
            P("fsdp", None),
            P("fsdp", None),
            P("fsdp", None),
            P("fsdp", None),
            P("fsdp"),
            P("fsdp", None),
            P("fsdp"),
            P("fsdp", None),
            P("fsdp"),
            P("fsdp", None),
            P("fsdp", None),
            P("fsdp", None),
        ),
        check_vma=False,
    )
```

profile of v0, /device:TPU:1, one launch (start us, length us, event | category | flops | bytes accessed | tf_op | source)
XLA Modules:
  0.0 1932.5 jit_solution(9073238078537246111)
XLA Ops:
  35.3 21.1 %all-gather.15.cloned.1.call-done = bf16[1024,512]{1,0:T(8,128)(2,1)} async-done(((bf16[512,512]{1,0:T(8,128)(2,1)}), bf16[1024,512]{1,0:T(8,128)(2,1)}) %all-gather.15.cloned.1.call-update) | async-done | bytes 1048592 | tf_op jit(solution)/shard_map/all_gather | solution.py:108
  66.7 24.4 %all-gather.17.cloned.1.call-done = bf16[1024,1024]{1,0:T(8,128)(2,1)} async-done(((bf16[512,1024]{1,0:T(8,128)(2,1)}), bf16[1024,1024]{1,0:T(8,128)(2,1)}) %all-gather.17.cloned.1.call-update) | async-done | bytes 2097168 | tf_op jit(solution)/shard_map/all_gather | solution.py:109
  105.1 9.9 all-to-all-done.1
  118.4 47.3 %while.34 = (s32[]{:T(128)}, f32[128,256]{1,0:T(8,128)S(1)}, f32[16,128,256]{2,1,0:T(8,128)S(1)}, f32[16,128,1]{1,2,0:T(1,128)}, f32[16,128]{1,0:T(8,128)}, /*index=5*/f32[16,128,256]{2,1,0:T(8,128)}, s32[]{:T(128)}, s32[]{:T(128)}) while((s32[]{:T(128)}, f32[128,256]{1,0:T(8,128)S(1)}, f32[16,128,256]{2,1,0:T(8,128)S(1)}, ...), condition=%wide.region_3.4_spmd.clone, body=%wide.region_2.3_spmd.clone.sunk | while | flops 131075 | bytes 658540 | solution.py:66
  209.9 26.3 %all-gather.23.cloned.1.call-done = bf16[1024,2816]{1,0:T(8,128)(2,1)} async-done(((bf16[512,2816]{1,0:T(8,128)(2,1)}), bf16[1024,2816]{1,0:T(8,128)(2,1)}) %all-gather.23.cloned.1.call-update) | async-done | bytes 5767184 | tf_op jit(solution)/shard_map/all_gather | solution.py:117
  242.2 70.0 %all-gather.25.cloned.1.call-done = bf16[1024,2816]{1,0:T(8,128)(2,1)} async-done(((bf16[512,2816]{1,0:T(8,128)(2,1)}), bf16[1024,2816]{1,0:T(8,128)(2,1)}) %all-gather.25.cloned.1.call-update) | async-done | bytes 5767184 | tf_op jit(solution)/shard_map/all_gather | solution.py:118
  318.3 70.0 %all-gather.27.cloned.1.call-done = bf16[2816,1024]{1,0:T(8,128)(2,1)} async-done(((bf16[1408,1024]{1,0:T(8,128)(2,1)}), bf16[2816,1024]{1,0:T(8,128)(2,1)}) %all-gather.27.cloned.1.call-update) | async-done | bytes 5767184 | tf_op jit(solution)/shard_map/all_gather | solution.py:119
  388.3 8.3 multiply_convert_fusion
  427.6 7.8 reshape.415
  435.4 7.7 reshape.417
  443.7 7.4 fusion.87
  451.1 18.2 reshape.419
  469.3 7.4 fusion.88
  476.8 18.4 reshape.420
  500.9 57.8 %while.35 = (s32[]{:T(128)}, f32[128,256]{1,0:T(8,128)S(1)}, f32[16,128]{1,0:T(8,128)}, f32[16,128,256]{2,1,0:T(8,128)}, f32[16,128,256]{2,1,0:T(8,128)}, /*inde...) while((s32[]{:T(128)}, f32[128,256]{1,0:T(8,128)S(1)}, ...), condition=%wide.region_10.11_spmd.clone, body=%wide.region_8.10_spmd.clone.sunk | while | flops 196484 | bytes 789644 | solution.py:66
  595.4 20.3 %reshape.421 = f32[2,1441792]{1,0:T(2,128)} reshape(f32[2816,1024]{1,0:T(8,128)} %fusion.89) | data formatting | bytes 23068672 | tf_op jit(solution)/shard_map/reshape | solution.py:278
  623.3 7.8 reshape.411
  690.9 111.8 %reshape.422 = f32[12872448]{0:T(1024)} reshape(f32[2,6436224]{1,0:T(2,128)} %constant_dynamic-update-slice_fusion.1) | data formatting | bytes 102979584 | tf_op jit(solution)/shard_map/reshape | solution.py:280
  802.6 813.6 %all-reduce.7 = bf16[12872448]{0:T(1024)(128)(2,1)} all-reduce(f32[12872448]{0:T(1024)} %reshape.422), channel_id=2, replica_groups=mesh['fsdp'=2,'seq'=16] {'fsdp','seq'}, use_global_device_ids=true, to_apply=%region_18.19.clone | all-reduce | flops 12872448 | bytes 77234688
  1622.6 13.1 dynamic-update-slice
  1643.9 230.8 %all-reduce.6.cloned.1.call-done = bf16[6436224]{0:T(1024)(128)(2,1)} async-done(((bf16[6436224]{0:T(1024)(128)(2,1)}), bf16[6436224]{0:T(1024)(128)(2,1)}) %all-reduce.6.cloned.1.call-update) | async-done | bytes 12872464
  1874.7 8.6 fusion.69
  1883.3 7.0 reshape.429
  1890.3 7.0 reshape.430
  (474 shorter events, 399.9 us)
Async XLA Ops:
  7.2 26.4 %all-gather.13.cloned.1.call-start = ((), (), s32[]{:S(2)}) async-start(), calls=%async_computation.6 | async-start | bytes 1572864 | tf_op jit(solution)/shard_map/all_gather | solution.py:107
  7.9 48.5 %all-gather.15.cloned.1.call-start = ((), (), s32[]{:S(2)}) async-start(), calls=%async_computation.7 | async-start | bytes 1572864 | tf_op jit(solution)/shard_map/all_gather | solution.py:108
  8.7 82.4 %all-gather.17.cloned.1.call-start = ((), (), s32[]{:S(2)}) async-start(), calls=%async_computation.8 | async-start | bytes 3145728 | tf_op jit(solution)/shard_map/all_gather | solution.py:109
  9.4 176.5 %all-gather.19.cloned.1.call-start = ((), (), s32[]{:S(2)}) async-start(), calls=%async_computation.9 | async-start | bytes 3145728 | tf_op jit(solution)/shard_map/all_gather | solution.py:113
  10.0 195.3 %all-gather.21.cloned.1.call-start = ((), (), s32[]{:S(2)}) async-start(), calls=%async_computation.10 | async-start | bytes 3145728 | tf_op jit(solution)/shard_map/all_gather | solution.py:115
  10.6 12.7 copy-start.53
  10.6 225.6 %all-gather.23.cloned.1.call-start = ((), (), s32[]{:S(2)}) async-start(), calls=%async_computation.11 | async-start | bytes 8650752 | tf_op jit(solution)/shard_map/all_gather | solution.py:117
  11.2 301.0 %all-gather.25.cloned.1.call-start = ((), (), s32[]{:S(2)}) async-start(), calls=%async_computation.12 | async-start | bytes 8650752 | tf_op jit(solution)/shard_map/all_gather | solution.py:118
  12.8 22.4 %copy-start.56 = (f32[256]{0:T(256)}, f32[256]{0:T(256)S(1)}, u32[]{:S(2)}) copy-start(f32[256]{0:T(256)S(1)} %rsqrt.33) | copy-start | bytes 3076
  27.6 63.5 %copy-start.7 = (bf16[256,1024]{1,0:T(8,128)(2,1)}, bf16[256,1024]{1,0:T(8,128)(2,1)S(1)}, u32[]{:S(2)}) copy-start(bf16[256,1024]{1,0:T(8,128)(2,1)S(1)} %fusion.20) | copy-start | bytes 1572868
  59.2 35.5 %all-to-all-start = ((bf16[16,64,384]{2,1,0:T(8,128)(2,1)}), bf16[16,64,384]{2,1,0:T(8,128)(2,1)S(1)}, u32[]{:S(2)}, u32[]{:S(2)}) async-start(bf16[16,64,384]{2,1,0:T(8,128)(2,1)} %bitcast.4), calls=%async_computation | async-start | bytes 1572864 | tf_op jit(solution)/shard_map/all_to_all | solution.py:163
  65.4 322.9 %all-gather.27.cloned.1.call-start = ((), (), s32[]{:S(2)}) async-start(), calls=%async_computation.13 | async-start | bytes 8650752 | tf_op jit(solution)/shard_map/all_gather | solution.py:119
  94.7 20.3 %all-to-all-start.1 = ((bf16[16,64,256]{2,1,0:T(8,128)(2,1)}), bf16[16,64,256]{2,1,0:T(8,128)(2,1)S(1)}, u32[]{:S(2)}, u32[]{:S(2)}) async-start(bf16[16,64,256]{2,1,0:T(8,128)(2,1)} %bitcast.10), calls=%async_computation.1 | async-start | bytes 1048576 | tf_op jit(solution)/shard_map/all_to_all | solution.py:164
  102.9 12.0 copy-start.25
  103.2 11.8 copy-start.9
  169.6 20.5 %all-to-all-start.2 = ((bf16[16,64,256]{2,1,0:T(8,128)(2,1)}), bf16[16,64,256]{2,1,0:T(8,128)(2,1)}, u32[]{:S(2)}, u32[]{:S(2)}) async-start(bf16[16,64,256]{2,1,0:T(8,128)(2,1)} %fusion.10), calls=%async_computation.2 | async-start | bytes 1048576 | tf_op jit(solution)/shard_map/all_to_all | solution.py:173
  417.5 77.7 %all-to-all-start.3 = ((bf16[16,64,256]{2,1,0:T(8,128)(2,1)}), bf16[16,64,256]{2,1,0:T(8,128)(2,1)}, u32[]{:S(2)}, u32[]{:S(2)}) async-start(bf16[16,64,256]{2,1,0:T(8,128)(2,1)} %bitcast.258), calls=%async_computation.3 | async-start | bytes 1048576 | tf_op jit(solution)/shard_map/all_to_all | solution.py:214
  564.3 20.3 %all-to-all-start.5 = ((bf16[16,64,256]{2,1,0:T(8,128)(2,1)}), bf16[16,64,256]{2,1,0:T(8,128)(2,1)}, u32[]{:S(2)}, u32[]{:S(2)}) async-start(bf16[16,64,256]{2,1,0:T(8,128)(2,1)} %fusion.11), calls=%async_computation.5 | async-start | bytes 1048576 | tf_op jit(solution)/shard_map/all_to_all | solution.py:224
  584.7 49.7 %all-to-all-start.4 = ((bf16[16,64,384]{2,1,0:T(8,128)(2,1)}), bf16[16,64,384]{2,1,0:T(8,128)(2,1)}, u32[]{:S(2)}, u32[]{:S(2)}) async-start(bf16[16,64,384]{2,1,0:T(8,128)(2,1)} %pad_maximum_fusion.1), calls=%async_computation.4 | async-start | bytes 1572864 | tf_op jit(solution)/shard_map/all_to_all | solution.py:217
  589.2 1285.5 %all-reduce.6.cloned.1.call-start = ((), (), s32[]{:S(2)}) async-start(), calls=%async_computation.14 | async-start | bytes 25747456
  595.4 20.3 %copy-start.18 = (bf16[1024,1024]{1,0:T(8,128)(2,1)S(1)}, bf16[1024,1024]{1,0:T(8,128)(2,1)}, u32[]{:S(2)}) copy-start(bf16[1024,1024]{1,0:T(8,128)(2,1)} %all-gather.19.cloned.1.call-done) | copy-start | bytes 6291460
  660.1 11.5 slice-start
  671.7 13.0 slice-start.6
  671.7 13.0 slice-start.7
  (71 other events, 294.0 us)
Sparse Core Ops, SparseCore 0:
  9.6 23.9 all-gather.12
  35.1 21.2 all-gather.14
  58.0 33.1 all-gather.16
  92.5 33.1 all-gather.18
  127.0 33.1 all-gather.20
  161.6 74.5 all-gather.22
  237.7 74.4 all-gather.24
  313.8 74.4 all-gather.26
  1635.8 238.8 all-reduce.5
where the time goes:
time: 1950 us; the launch traced here: 1930 us
  blocking collectives  835 us (43%)
  waiting for transfers between devices  465 us (24%)
  local copies, waits for them, and re-layouts  403 us (21%)
  matrix products  119 us (6%)
  other arithmetic  59.8 us (3%)
  starting transfers between devices  34.3 us (2%)
    unnamed x1, blocking collectives  814 us
    unnamed x10, waiting for transfers between devices  236 us
    reshape x1, local copies, waits for them, and re-layouts, per_device(): packed.reshape(-1)  112 us
    reshape x13, local copies, waits for them, and re-layouts, per_device(): gradient.reshape(fsdp_count, -1)  89.3 us
    all_gather x1, waiting for transfers between devices, per_device(): lax.all_gather(feed_up, 'fsdp', axis=0, tiled=True)  70 us
    all_gather x1, waiting for transfers between devices, per_device(): lax.all_gather(feed_down, 'fsdp', axis=0, tiled=True)  70 us
    unnamed x182, local copies, waits for them, and re-layouts  60 us
    dynamic_update_slice x32, local copies, waits for them, and re-layouts, span_mix(): _, before = lax.scan(advance, initial, (span_fade, updates))  40.6 us
  transfers between devices with their start and end apart: 15, of which 9 were waited for; matrix products, arithmetic and copies ran while one was open for 13% of the time, Pallas kernels for 0%

commit v1 on v0

v1 whole, which is shorter than its diff:
```python
import functools

import jax
import jax.numpy as jnp
from jax import lax
from jax.experimental import pallas as pl
from jax.experimental.pallas import tpu as pltpu
from jax.sharding import PartitionSpec as P

H = 4
DK = 128
DV = 256
SPAN = 64


epsilon = 1e-06
head_floor = 0.25
gate_scale = 16.0
highest = lax.Precision.HIGHEST
bf16 = jnp.bfloat16
f32 = jnp.float32


def rms_scale(values, scale_gain):
    return (
        values * lax.rsqrt(jnp.mean(values * values, axis=-1, keepdims=True) + epsilon) * scale_gain
    )


def head_scale(values, scale_gain):
    return (
        values
        * lax.rsqrt(jnp.maximum(jnp.mean(values * values, axis=-1, keepdims=True), head_floor))
        * scale_gain
    )


def swiglu(gate_part, up_part):
    return jax.nn.silu(gate_part) * up_part


def head_mix(mixed, out_gate, head_gain):
    row_count = mixed.shape[0]
    normed = head_scale(mixed, head_gain)
    return (normed * jax.nn.silu(out_gate.reshape(mixed.shape))).reshape(row_count, -1)


def mat_product(left, right):
    return jnp.dot(left, right, preferred_element_type=f32)


def cross_rows(left, right):
    return lax.dot_general(left, right, (((0,), (0,)), ((), ())), preferred_element_type=f32)


def back_product(left, right):
    return lax.dot_general(left, right, (((1,), (1,)), ((), ())), preferred_element_type=f32)


def fine(left, right, contract):
    return lax.dot_general(
        left, right, (((contract[0],), (contract[1],)), ((), ())),
        precision=highest, preferred_element_type=f32,
    )


def triangle():
    rows = lax.broadcasted_iota(jnp.int32, (SPAN, SPAN), 0)
    cols = lax.broadcasted_iota(jnp.int32, (SPAN, SPAN), 1)
    return rows >= cols


def block_terms(q_ref, k_ref, g_ref, head):
    cols = slice(head * DK, (head + 1) * DK)
    lower = jnp.where(triangle(), 1.0, 0.0).astype(bf16)
    c = jnp.dot(lower, g_ref[:, cols], preferred_element_type=f32)
    e = c[SPAN - 1 : SPAN, :]
    qt = q_ref[:, cols].astype(f32) * DK ** (-0.5) * jnp.exp(c)
    keys = k_ref[:, cols].astype(f32)
    return c, e, qt, keys * jnp.exp(-c), keys * jnp.exp(e - c)


def local_kernel(q_ref, k_ref, g_ref, v_ref, inside_ref, update_ref, fade_ref):
    for head in range(H):
        wide = slice(head * DV, (head + 1) * DV)
        c, e, qt, kt, kl = block_terms(q_ref, k_ref, g_ref, head)
        v = v_ref[:, wide].astype(f32)
        scores = jnp.where(triangle(), fine(qt, kt, (1, 1)), 0.0)
        inside_ref[:, wide] = fine(scores, v, (1, 0))
        update_ref[head] = fine(kl, v, (0, 0)).astype(bf16)
        fade_ref[0, head : head + 1, :] = jnp.exp(e)


def outside_kernel(q_ref, k_ref, g_ref, inside_ref, state_ref, mixed_ref):
    for head in range(H):
        wide = slice(head * DV, (head + 1) * DV)
        c, e, qt, kt, kl = block_terms(q_ref, k_ref, g_ref, head)
        state = state_ref[head].astype(f32)
        mixed_ref[:, wide] = (inside_ref[:, wide] + fine(qt, state, (1, 0))).astype(bf16)


def back_state_kernel(q_ref, k_ref, g_ref, do_ref, update_ref):
    for head in range(H):
        wide = slice(head * DV, (head + 1) * DV)
        c, e, qt, kt, kl = block_terms(q_ref, k_ref, g_ref, head)
        update_ref[head] = fine(qt, do_ref[:, wide].astype(f32), (0, 0)).astype(bf16)


def back_kernel(
    q_ref, k_ref, g_ref, v_ref, do_ref, state_ref, after_ref, dq_ref, dk_ref, dg_ref, dv_ref
):
    mask = triangle()
    upper = jnp.where(
        lax.broadcasted_iota(jnp.int32, (SPAN, SPAN), 0)
        <= lax.broadcasted_iota(jnp.int32, (SPAN, SPAN), 1),
        1.0,
        0.0,
    )
    last = lax.broadcasted_iota(jnp.int32, (SPAN, DK), 0) == SPAN - 1
    for head in range(H):
        wide = slice(head * DV, (head + 1) * DV)
        cols = slice(head * DK, (head + 1) * DK)
        c, e, qt, kt, kl = block_terms(q_ref, k_ref, g_ref, head)
        v = v_ref[:, wide].astype(f32)
        do = do_ref[:, wide].astype(f32)
        state = state_ref[head].astype(f32)
        after = after_ref[head].astype(f32)
        scores = jnp.where(mask, fine(qt, kt, (1, 1)), 0.0)
        d_scores = jnp.where(mask, fine(do, v, (1, 1)), 0.0)
        dv_ref[:, wide] = (fine(scores, do, (0, 0)) + fine(kl, after, (1, 0))).astype(bf16)
        dqt = fine(d_scores, kt, (1, 0)) + fine(do, state, (1, 1))
        dkt = fine(d_scores, qt, (0, 0))
        dkl = fine(v, after, (1, 1))
        dq_ref[:, cols] = (dqt * (DK ** (-0.5) * jnp.exp(c))).astype(bf16)
        dk_ref[:, cols] = (dkt * jnp.exp(-c) + dkl * jnp.exp(e - c)).astype(bf16)
        tail = kl * dkl
        ones = jnp.ones((8, DV), f32)
        fade_grad = fine(ones, after * state, (1, 1))[0:1, :]
        de = jnp.sum(tail, axis=0, keepdims=True) + jnp.exp(e) * fade_grad
        dc = qt * dqt - kt * dkt - tail + jnp.where(last, de, 0.0)
        dg_ref[:, cols] = fine(upper, dc, (1, 0)).astype(bf16)


def row_spec(width):
    return pl.BlockSpec((SPAN, width), lambda i: (i, 0))


def head_spec():
    return pl.BlockSpec((H, DK, DV), lambda i: (i, 0, 0))


def block_call(kernel, seq_count, in_specs, out_specs, out_shape, flops):
    return pl.pallas_call(
        kernel,
        grid=(seq_count,),
        in_specs=in_specs,
        out_specs=out_specs,
        out_shape=out_shape,
        compiler_params=pltpu.CompilerParams(vmem_limit_bytes=24 * 1024 * 1024),
        cost_estimate=pl.CostEstimate(
            flops=flops * seq_count * H, bytes_accessed=4 * 1024 * 1024, transcendentals=0
        ),
    )


class Links:
    def __init__(self):
        self.fsdp = lax.axis_index("fsdp")
        self.seq = lax.axis_index("seq")
        self.seq_count = lax.axis_size("seq")
        self.bits = self.seq_count.bit_length() - 1

    def own(self, axis):
        return self.fsdp if axis == "fsdp" else lax.rem(lax.div(self.seq, 1 << axis), 2)

    def swap(self, array, axis):
        if axis == "fsdp":
            return lax.ppermute(array, "fsdp", [(0, 1), (1, 0)])
        return lax.ppermute(
            array, "seq", [(i, i ^ (1 << axis)) for i in range(self.seq_count)]
        )

    def shift(self, array, steps):
        moves = [
            (i, i + steps) for i in range(self.seq_count) if 0 <= i + steps < self.seq_count
        ]
        return lax.ppermute(array, "seq", moves)


def pick(array, index, axis=0):
    return lax.dynamic_index_in_dim(array, index, axis, keepdims=False)


def in_order(bit, own, other, axis):
    size = own.shape[axis]
    shape = list(own.shape)
    shape[axis] = 2 * size
    whole = jnp.zeros(shape, own.dtype)
    whole = lax.dynamic_update_slice_in_dim(whole, own, bit * size, axis)
    return lax.dynamic_update_slice_in_dim(whole, other, (1 - bit) * size, axis)


def gather_weight(links, mine, bits):
    rows = mine.shape[0] >> len(bits)
    place = sum(links.own(bit) << i for i, bit in enumerate(bits))
    piece = lax.dynamic_slice_in_dim(mine, place * rows, rows, 0)
    held = [(0, links.swap(piece, "fsdp"))]
    for i, bit in enumerate(bits):
        held = held + [(rel ^ (1 << i), links.swap(x, bit)) for rel, x in held]
    whole = jnp.zeros((2 * mine.shape[0],) + mine.shape[1:], mine.dtype)
    whole = lax.dynamic_update_slice_in_dim(whole, mine, links.fsdp * mine.shape[0], 0)
    base = (1 - links.fsdp) * mine.shape[0]
    for rel, x in held:
        whole = lax.dynamic_update_slice_in_dim(
            whole, x, base + jnp.bitwise_xor(place, rel) * rows, 0
        )
    return whole


def prefix_states(links, update, fade, backward):
    heads = update.shape[0]

    def position(bit):
        return 1 - links.own(bit) if backward else links.own(bit)

    def meet(bit, t, f):
        count = t.shape[0] // 2
        mine = links.own(bit)
        t2 = t.reshape((2, count) + t.shape[1:])
        other_t = links.swap(pick(t2, 1 - mine).astype(bf16), bit).astype(f32)
        other_f = links.swap(f, bit)
        f2 = f.reshape((2, count) + f.shape[1:])
        of2 = other_f.reshape(f2.shape)
        own_t, own_f = pick(t2, mine).astype(f32), pick(f2, mine)
        other_f = pick(of2, mine)
        second = position(bit) == 1
        first_t = jnp.where(second, other_t, own_t)
        first_f = jnp.where(second, other_f, own_f)
        last_t = jnp.where(second, own_t, other_t)
        last_f = jnp.where(second, own_f, other_f)
        return first_t, first_f, first_t * last_f[..., None] + last_t, first_f * last_f

    t0, f0, t, f = meet(0, update, fade)
    t1, f1, t, f = meet(1, t, f)
    sign = -1 if backward else 1
    t = links.shift(t.astype(bf16), 4 * sign).astype(f32)
    f = links.shift(f, 4 * sign)
    reach = 1
    groups = links.seq_count // 4
    while reach < groups - 1:
        got_t = links.shift(t.astype(bf16), 4 * reach * sign).astype(f32)
        got_f = links.shift(f, 4 * reach * sign)
        t = t + f[..., None] * got_t
        f = f * got_f
        reach *= 2

    def part(bit, before, first_t, first_f):
        later = before * first_f[..., None] + first_t
        second = position(bit) == 1
        mine = jnp.where(second, later, before).astype(bf16)
        other = links.swap(jnp.where(second, before, later).astype(bf16), bit)
        return in_order(links.own(bit), mine, other, 0)

    t = part(1, t, t1, f1)
    return part(0, t.astype(f32), t0, f0)


def sum_rows(links, partial, order):
    rows, cols = partial.shape
    axes = ["fsdp"] + list(range(1, links.bits))
    shares = 1 << len(axes)
    data = partial.reshape([2] * len(axes) + [rows // shares, cols])
    left = list(axes)
    for axis in order:
        dim = left.index(axis)
        mine = links.own(axis)
        got = links.swap(pick(data, 1 - mine, dim), axis)
        data = (pick(data, mine, dim).astype(f32) + got.astype(f32)).astype(bf16)
        left.remove(axis)
    data = data.reshape((rows // shares, cols))
    return data


def share_rows(links, data):
    for axis in range(links.bits - 1, 0, -1):
        data = in_order(links.own(axis), data, links.swap(data, axis), 0)
    return data


def columns_of_cores(links, data):
    other = links.swap(data, 0)
    first = links.own(0) == 0
    return jnp.where(first, data, other).astype(f32), jnp.where(first, other, data).astype(f32)


def half_columns(links, array, parts):
    mine = links.own(0)
    ours, theirs = [], []
    offset = 0
    for width in parts:
        piece = array[:, offset : offset + width]
        ours.append(lax.dynamic_slice_in_dim(piece, mine * (width // 2), width // 2, 1))
        theirs.append(lax.dynamic_slice_in_dim(piece, (1 - mine) * (width // 2), width // 2, 1))
        offset += width
    return jnp.concatenate(ours, axis=1), jnp.concatenate(theirs, axis=1)


def both_cores(links, array):
    return jnp.concatenate((array, links.swap(array, 0)), axis=0)


def wide_grad(links, left_both, right, parts):
    ours, theirs = half_columns(links, right, parts)
    right_both = jnp.concatenate((ours, links.swap(theirs, 0)), axis=0)
    return cross_rows(left_both, right_both).astype(bf16)


def per_device(
    inputs,
    mixer_gain,
    query_weight,
    key_weight,
    value_weight,
    decay_down,
    decay_up,
    decay_bias,
    outgate_weight,
    head_gain,
    output_weight,
    feed_gain,
    feed_gate,
    feed_up,
    feed_down,
    cotangent,
):
    links = Links()
    seq_count, seg_rows, width = inputs.shape
    row_count = seq_count * seg_rows
    rank = decay_down.shape[1]
    hidden_width = feed_gate.shape[1]
    key_cols, value_cols = H * DK, H * DV

    small = (mixer_gain, decay_down, decay_up, decay_bias, head_gain, feed_gain)
    packed = jnp.concatenate([piece.reshape(-1) for piece in small])
    packed_other = links.swap(packed, "fsdp")
    low_half = jnp.where(links.fsdp == 0, packed, packed_other)
    high_half = jnp.where(links.fsdp == 0, packed_other, packed)
    whole_small = []
    offset = 0
    for piece in small:
        parts = [half[offset : offset + piece.size].reshape(piece.shape) for half in (low_half, high_half)]
        whole_small.append(jnp.concatenate(parts, axis=0))
        offset += piece.size
    full_mixer_gain, full_down, full_up_rank, full_bias, full_head_gain, full_feed_gain = whole_small

    in_widths = (key_cols, key_cols, value_cols, value_cols)
    near = [1, 0]
    far = [1, 2, 0]
    full_in = gather_weight(
        links,
        jnp.concatenate((query_weight, key_weight, value_weight, outgate_weight), axis=1),
        near,
    )
    full_output = gather_weight(links, output_weight, near)
    full_feed_gate = gather_weight(links, feed_gate, far)
    full_feed_up = gather_weight(links, feed_up, far)
    full_feed_down = gather_weight(links, feed_down, far)

    residual_in = inputs.reshape(row_count, width).astype(f32)
    normed_full, first_pull = jax.vjp(rms_scale, residual_in, full_mixer_gain.astype(f32))
    normed = normed_full.astype(bf16)
    projected = mat_product(normed, full_in)
    query = projected[:, :key_cols].astype(bf16)
    keys = projected[:, key_cols : 2 * key_cols].astype(bf16)
    values = projected[:, 2 * key_cols : 2 * key_cols + value_cols].astype(bf16)
    out_gate = projected[:, 2 * key_cols + value_cols :]
    ranked = mat_product(normed, full_down).astype(bf16)
    decay_in = mat_product(ranked, full_up_rank) + full_bias.astype(f32)
    decay = (jax.nn.log_sigmoid(decay_in) / gate_scale).astype(bf16)

    qkg_specs = [row_spec(key_cols)] * 3
    state_shape = jax.ShapeDtypeStruct((seq_count * H, DK, DV), bf16)
    block_flops = 2 * SPAN * DK * DV * 6
    inside, update, fade = block_call(
        local_kernel,
        seq_count,
        qkg_specs + [row_spec(value_cols)],
        [row_spec(value_cols), head_spec(), pl.BlockSpec((1, H, DK), lambda i: (i, 0, 0))],
        [
            jax.ShapeDtypeStruct((row_count, value_cols), f32),
            state_shape,
            jax.ShapeDtypeStruct((seq_count, H, DK), f32),
        ],
        2 * block_flops,
    )(query, keys, decay, values)
    fade = fade.reshape(seq_count * H, DK)
    state = prefix_states(links, update, fade, False)
    mixed = block_call(
        outside_kernel,
        seq_count,
        qkg_specs + [row_spec(value_cols), head_spec()],
        row_spec(value_cols),
        jax.ShapeDtypeStruct((row_count, value_cols), bf16),
        block_flops,
    )(query, keys, decay, inside, state)
    mixed_rows = mixed.reshape(row_count, H, DV).astype(f32)
    gated_full, head_pull = jax.vjp(head_mix, mixed_rows, out_gate, full_head_gain.astype(f32))
    gated = gated_full.astype(bf16)
    middle = residual_in + mat_product(gated, full_output)
    second_full, second_pull = jax.vjp(rms_scale, middle, full_feed_gain.astype(f32))
    second_norm = second_full.astype(bf16)
    gate_part = mat_product(second_norm, full_feed_gate)
    up_part = mat_product(second_norm, full_feed_up)
    hidden_full, act_pull = jax.vjp(swiglu, gate_part, up_part)
    hidden = hidden_full.astype(bf16)
    final = middle + mat_product(hidden, full_feed_down)
    output = final.astype(bf16).reshape(seq_count, seg_rows, width)

    d_down = cotangent.reshape(row_count, width)
    seq_grad = d_down.astype(f32)
    d_hidden = back_product(d_down, full_feed_down)
    d_gate_full, d_up_full = act_pull(d_hidden)
    d_gate = d_gate_full.astype(bf16)
    d_up = d_up_full.astype(bf16)
    d_second = back_product(d_gate, full_feed_gate) + back_product(d_up, full_feed_up)
    d_middle_norm, grad_feed_gain = second_pull(d_second)
    d_middle = seq_grad + d_middle_norm
    d_branch = d_middle.astype(bf16)
    d_gated = back_product(d_branch, full_output)
    d_mixed, d_outgate_full, grad_head_gain = head_pull(d_gated)
    d_mixed_low = d_mixed.astype(bf16).reshape(row_count, value_cols)
    d_outgate = d_outgate_full.astype(bf16)

    yxz = ["fsdp"] + list(range(1, links.bits))
    normed_both = both_cores(links, normed)
    second_both = both_cores(links, second_norm)
    hidden_both = both_cores(links, hidden)
    gated_both = both_cores(links, gated)
    sum_down = sum_rows(links, wide_grad(links, hidden_both, d_down, (width,)), yxz)
    sum_gate = sum_rows(links, wide_grad(links, second_both, d_gate, (hidden_width,)), yxz)
    sum_up = sum_rows(links, wide_grad(links, second_both, d_up, (hidden_width,)), yxz)
    sum_output = sum_rows(links, wide_grad(links, gated_both, d_branch, (width,)), yxz)
    sum_outgate = sum_rows(links, wide_grad(links, normed_both, d_outgate, (value_cols,)), yxz)

    back_update = block_call(
        back_state_kernel,
        seq_count,
        qkg_specs + [row_spec(value_cols)],
        head_spec(),
        state_shape,
        block_flops,
    )(query, keys, decay, d_mixed_low)
    after = prefix_states(links, back_update, fade, True)
    d_query, d_keys, d_decay, d_values = block_call(
        back_kernel,
        seq_count,
        qkg_specs + [row_spec(value_cols)] * 2 + [head_spec()] * 2,
        [row_spec(key_cols)] * 3 + [row_spec(value_cols)],
        [jax.ShapeDtypeStruct((row_count, key_cols), bf16)] * 3
        + [jax.ShapeDtypeStruct((row_count, value_cols), bf16)],
        4 * block_flops,
    )(query, keys, decay, values, d_mixed_low, state, after)

    d_decay_in = d_decay.astype(f32) * jax.nn.sigmoid(-decay_in) / gate_scale
    grad_decay_bias = jnp.sum(d_decay_in, axis=0)
    grad_decay_up = lax.dot_general(
        ranked.astype(f32), d_decay_in, (((0,), (0,)), ((), ())), precision=highest
    )
    d_ranked = lax.dot_general(
        d_decay_in, full_up_rank.astype(f32), (((1,), (1,)), ((), ())), precision=highest
    ).astype(bf16)
    d_qkv = jnp.concatenate((d_query, d_keys, d_values), axis=1)
    sum_qkv = sum_rows(links, wide_grad(links, normed_both, d_qkv, in_widths[:3]), yxz)
    grad_decay_down = cross_rows(normed, d_ranked)
    d_normed = back_product(
        jnp.concatenate((d_qkv, d_outgate), axis=1), full_in
    ) + back_product(d_ranked, full_down)
    d_input_norm, grad_mixer_gain = first_pull(d_normed)
    input_grad = (d_middle + d_input_norm).reshape(seq_count, seg_rows, width)

    small_grads = (
        grad_mixer_gain, grad_decay_down, grad_decay_up, grad_decay_bias, grad_head_gain,
        grad_feed_gain,
    )
    total = jnp.concatenate([grad.reshape(2, -1) for grad in small_grads], axis=1)
    total = pick(total, links.fsdp) + links.swap(pick(total, 1 - links.fsdp), "fsdp")
    for bit in range(links.bits):
        total = total + links.swap(total, bit)
    small_out = []
    offset = 0
    for grad in small_grads:
        size = grad.size // 2
        small_out.append(
            total[offset : offset + size].reshape((grad.shape[0] // 2,) + grad.shape[1:])
        )
        offset += size
    out_mixer_gain, out_decay_down, out_decay_up, out_bias, out_head_gain, out_feed_gain = small_out

    def finish(shares, parts):
        low, high = columns_of_cores(links, share_rows(links, shares))
        offset = 0
        outs = []
        for part in parts:
            half = part // 2
            outs.append(
                jnp.concatenate(
                    (low[:, offset : offset + half], high[:, offset : offset + half]), axis=1
                )
            )
            offset += half
        return outs

    (out_down,) = finish(sum_down, (width,))
    (out_gate_w,) = finish(sum_gate, (hidden_width,))
    (out_up_w,) = finish(sum_up, (hidden_width,))
    (out_output,) = finish(sum_output, (width,))
    (out_outgate,) = finish(sum_outgate, (value_cols,))
    out_query, out_key, out_value = finish(sum_qkv, in_widths[:3])
    return (
        output,
        input_grad,
        out_mixer_gain,
        out_query,
        out_key,
        out_value,
        out_decay_down,
        out_decay_up,
        out_bias,
        out_outgate,
        out_head_gain,
        out_output,
        out_feed_gain,
        out_gate_w,
        out_up_w,
        out_down,
    )


def solution(mesh):
    rows = P("fsdp", None)
    gains = P("fsdp")
    tokens = P("fsdp", "seq", None)
    weights = (gains, rows, rows, rows, rows, rows, gains, rows, gains, rows, gains, rows, rows, rows)
    return jax.shard_map(
        per_device,
        mesh=mesh,
        in_specs=(tokens,) + weights + (tokens,),
        out_specs=(tokens, tokens) + weights,
        check_vma=False,
    )
```

time: 1950 us -> 602 us (0.31)
  blocking collectives: 835 us -> 0 us
  local copies, waits for them, and re-layouts: 403 us -> 99.5 us
  waiting for transfers between devices: 465 us -> 211 us
  starting transfers between devices: 34.3 us -> 137 us
  matrix products: 119 us -> 59.1 us
  Pallas kernels: 0 us -> 29.8 us
    unnamed x1 -> x0, blocking collectives: 814 us -> none
    unnamed x10 -> x0, waiting for transfers between devices: 236 us -> none
    reshape x30 -> x11, local copies, waits for them, and re-layouts: 232 us -> 7.08 us  [the longest x1 2.67 us: head_mix(): (normed * jax.nn.silu(out_gate.reshape(mixed.shape))).reshape(row_count, -1)]
    all_gather x8 -> x0, waiting for transfers between devices: 216 us -> none  [the longest x1 70 us: per_device(): lax.all_gather(feed_up, 'fsdp', axis=0, tiled=True)]
    ppermute x0 -> x117, waiting for transfers between devices: none -> 211 us  [the longest x94 189 us: swap(): lax.ppermute(array, 'seq', [(i, i ^ 1 << axis) for i in range(self.seq_co...]
    ppermute x0 -> x117, starting transfers between devices: none -> 137 us  [the longest x94 105 us: swap(): lax.ppermute(array, 'seq', [(i, i ^ 1 << axis) for i in range(self.seq_co...]
    unnamed x182 -> x191, local copies, waits for them, and re-layouts: 60 us -> 18.1 us
    all_to_all x6 -> x0, starting transfers between devices: 33.7 us -> none  [the longest x1 6.2 us: per_device(): lax.all_to_all(value_send, 'seq', split_axis=0, concat_axis=0, tiled=True)]
  transfers between devices with their start and end apart: 15 -> 117, of which waited for: 9 -> 49; matrix products, arithmetic and copies ran while one was open for 13% -> 33% of each run, Pallas kernels for 0% -> 5%
where the time goes in v1:
time: 602 us; the launch traced here: 593 us
  waiting for transfers between devices  211 us (35%)
  starting transfers between devices  137 us (23%)
  local copies, waits for them, and re-layouts  99.5 us (17%)
  matrix products  59.1 us (10%)
  other arithmetic  52.1 us (9%)
  Pallas kernels  29.8 us (5%)
    ppermute x94, waiting for transfers between devices, swap(): lax.ppermute(array, 'seq', [(i, i ^ 1 << axis) for i in range(self.seq_co...  189 us
    ppermute x94, starting transfers between devices, swap(): lax.ppermute(array, 'seq', [(i, i ^ 1 << axis) for i in range(self.seq_co...  105 us
    dynamic_update_slice x32, local copies, waits for them, and re-layouts, gather_weight(): lax.dynamic_update_slice_in_dim(whole, x, base + jnp.bitwise_xor(place, r...  27.7 us
    dot_general x7, matrix products, mat_product(): return jnp.dot(left, right, preferred_element_type=f32)  26.1 us
    ppermute x10, starting transfers between devices, shift(): return lax.ppermute(array, 'seq', moves)  22.8 us
    unnamed x191, local copies, waits for them, and re-layouts  18.1 us
    dot_general x6, matrix products, back_product(): lax.dot_general(left, right, (((1,), (1,)), ((), ())), preferred_element_...  17.8 us
    concatenate x8, other arithmetic, finish(): jnp.concatenate((low[:, offset:offset + half], high[:, offset:offset + ha...  16.1 us
  transfers between devices with their start and end apart: 117, of which 49 were waited for; matrix products, arithmetic and copies ran while one was open for 33% of the time, Pallas kernels for 5%

profile of v1, /device:TPU:1, one launch (start us, length us, event | category | flops | bytes accessed | tf_op | source)
XLA Modules:
  0.0 592.7 jit_solution(14708458732756392298)
XLA Ops:
  74.3 7.0 %collective-permute-done.37 = bf16[176,1024]{1,0:T(8,128)(2,1)S(1)} collective-permute-done((bf16[176,1024]{1,0:T(8,128)(2,1)}, bf16[176,1024]{1,0:T(8,128)(2,1)S(1)}, u32[]{:S(2)}, u32[]{:S(2)}) %collective-permute-start.37) | collective-permute-done | bytes 360480 | tf_op jit(solution)/shard_map/ppermute | solution.py:179
  92.0 5.9 %collective-permute-done.30 = bf16[64,2816]{1,0:T(8,128)(2,1)S(1)} collective-permute-done((bf16[64,2816]{1,0:T(8,128)(2,1)}, bf16[64,2816]{1,0:T(8,128)(2,1)S(1)}, u32[]{:S(2)}, u32[]{:S(2)}) %collective-permute-start.30) | collective-permute-done | bytes 360480 | tf_op jit(solution)/shard_map/ppermute | solution.py:179
  119.6 6.7 %collective-permute-done.23 = bf16[64,2816]{1,0:T(8,128)(2,1)S(1)} collective-permute-done((bf16[64,2816]{1,0:T(8,128)(2,1)S(1)}, bf16[64,2816]{1,0:T(8,128)(2,1)S(1)}, u32[]{:S(2)}, u32[]{:S(2)}) %collective-permute-start.23) | collective-permute-done | bytes 360480 | tf_op jit(solution)/shard_map/ppermute | solution.py:179
  129.6 6.3 %collective-permute-done.2 = bf16[128,3072]{1,0:T(8,128)(2,1)S(1)} collective-permute-done((bf16[128,3072]{1,0:T(8,128)(2,1)}, bf16[128,3072]{1,0:T(8,128)(2,1)S(1)}, u32[]{:S(2)}, u32[]{:S(2)}) %collective-permute-start.2) | collective-permute-done | bytes 786464 | tf_op jit(solution)/shard_map/ppermute | solution.py:179
  143.0 6.4 %fusion.149 = (bf16[256,3072]{1,0:T(8,128)(2,1)S(1)}, f32[256,3072]{1,0:T(8,128)}) fusion(bf16[256,1024]{1,0:T(8,128)(2,1)} %fusion.63, bf16[1024,3072]{1,0:T(8,128)(2,1)} %constant_dynamic-update-slice_fusion.72), kind=kOutput, calls=%fused_computation.410 | convolution fusion | flops 1611399168 | bytes 11534336 | tf_op jit(solution)/shard_map/dot_general | solution.py:49
  149.5 8.3 %shard_map.279 = (f32[256,1024]{1,0:T(8,128)S(1)}, bf16[16,128,256]{2,1,0:T(8,128)(2,1)S(1)}, f32[4,4,128]{2,1,0:T(4,128)S(1)}) custom-call(bf16[256,512]{1,0:T(8,128)(2,1)S(1)} %get-tuple-element.131.q_ref, bf16[256,512]{1,0:T(8,128)(2,1)S(1)} %get-tuple-element.130.k_ref, bf16[256,512]{1,0:T(8,128)(2,1)S(1)} %get-tuple-element.167.g_ref, ...), custom_call_target="tpu_custom_call" | custom-call | flops 805306368 | bytes 4194304 | tf_op jit(solution)/shard_map/pallas_call | solution.py:384
  163.6 5.6 collective-permute-done.8
  194.1 5.5 collective-permute-start.13
  199.6 5.9 convolution_bitcast_fusion
  293.5 7.8 %collective-permute-done.70 = bf16[2,2,2,64,512]{4,3,2,1,0:T(8,128)(2,1)S(1)} collective-permute-done((bf16[2,2,2,64,512]{4,3,2,1,0:T(8,128)(2,1)S(1)}, bf16[2,2,2,64,512]{4,3,2,1,0:T(8,128)(2,1)S(1)}, u32[]{:S(2)}, u32[]{:S(2)}) %collective-permute-start.70) | collective-permute-done | bytes 524320 | tf_op jit(solution)/shard_map/ppermute | solution.py:178
  325.3 6.0 %collective-permute-done.49 = bf16[4,128,256]{2,1,0:T(8,128)(2,1)S(1)} collective-permute-done((bf16[4,128,256]{2,1,0:T(8,128)(2,1)S(1)}, bf16[4,128,256]{2,1,0:T(8,128)(2,1)S(1)}, u32[]{:S(2)}, u32[]{:S(2)}) %collective-permute-start.49) | collective-permute-done | bytes 262176 | tf_op jit(solution)/shard_map/ppermute | solution.py:187
  354.1 6.6 %collective-permute-done.84 = bf16[64,512]{1,0:T(8,128)(2,1)S(1)} collective-permute-done((bf16[64,512]{1,0:T(8,128)(2,1)S(1)}, bf16[64,512]{1,0:T(8,128)(2,1)S(1)}, u32[]{:S(2)}, u32[]{:S(2)}) %collective-permute-start.84) | collective-permute-done | bytes 65568 | tf_op jit(solution)/shard_map/ppermute | solution.py:179
  370.8 10.2 %collective-permute-start.77 = (bf16[512,512]{1,0:T(8,128)(2,1)S(1)}, bf16[512,512]{1,0:T(8,128)(2,1)S(1)}, u32[]{:S(2)}, u32[]{:S(2)}) collective-permute-start(bf16[512,512]{1,0:T(8,128)(2,1)S(1)} %constant_dynamic-update-slice_fusion.24), channel_id=1, source_target_pairs={{0,1},{1,0},{2,3},{3,2},{4,5},{5,4},{6,7},{7,6},{8,9},{9,8},{10,11... | collective-permute-start | bytes 1572872 | tf_op jit(solution)/shard_map/ppermute | solution.py:179
  391.2 14.6 %shard_map.282 = (bf16[256,512]{1,0:T(8,128)(2,1)S(1)}, bf16[256,512]{1,0:T(8,128)(2,1)S(1)}, bf16[256,512]{1,0:T(8,128)(2,1)S(1)}, bf16[256,1024]{1,0:T(8,128)(2,1)S(1)}) custom-call(bf16[256,512]{1,0:T(8,128)(2,1)S(1)} %get-tuple-element.131.q_ref, bf16[256,512]{1,0:T(8,128)(2,1)S(1)} %get-tuple-element.130.k_ref, ...), custom_call_target="tpu_custom_call" | custom-call | flops 1610612736 | bytes 4194304 | tf_op jit(solution)/shard_map/pallas_call | solution.py:454
  453.1 11.4 %collective-permute-done.101 = bf16[2,64,1408]{2,1,0:T(8,128)(2,1)S(1)} collective-permute-done((bf16[2,64,1408]{2,1,0:T(8,128)(2,1)S(1)}, bf16[2,64,1408]{2,1,0:T(8,128)(2,1)S(1)}, u32[]{:S(2)}, u32[]{:S(2)}) %collective-permute-start.101) | collective-permute-done | bytes 360480 | tf_op jit(solution)/shard_map/ppermute | solution.py:179
  467.2 9.6 %collective-permute-done.102 = bf16[64,1408]{1,0:T(8,128)(2,1)S(1)} collective-permute-done((bf16[64,1408]{1,0:T(8,128)(2,1)S(1)}, bf16[64,1408]{1,0:T(8,128)(2,1)S(1)}, u32[]{:S(2)}, u32[]{:S(2)}) %collective-permute-start.102) | collective-permute-done | bytes 180256 | tf_op jit(solution)/shard_map/ppermute | solution.py:179
  477.0 7.5 %collective-permute-done.94 = bf16[64,1408]{1,0:T(8,128)(2,1)S(1)} collective-permute-done((bf16[64,1408]{1,0:T(8,128)(2,1)S(1)}, bf16[64,1408]{1,0:T(8,128)(2,1)S(1)}, u32[]{:S(2)}, u32[]{:S(2)}) %collective-permute-start.94) | collective-permute-done | bytes 180256 | tf_op jit(solution)/shard_map/ppermute | solution.py:179
  496.0 7.3 %collective-permute-done.104 = bf16[128,1408]{1,0:T(8,128)(2,1)S(1)} collective-permute-done((bf16[128,1408]{1,0:T(8,128)(2,1)S(1)}, bf16[128,1408]{1,0:T(8,128)(2,1)S(1)}, u32[]{:S(2)}, u32[]{:S(2)}) %collective-permute-start.104) | collective-permute-done | bytes 360480 | tf_op jit(solution)/shard_map/ppermute | solution.py:179
  503.7 7.3 %collective-permute-done.111 = bf16[2,176,512]{2,1,0:T(8,128)(2,1)S(1)} collective-permute-done((bf16[2,176,512]{2,1,0:T(8,128)(2,1)S(1)}, bf16[2,176,512]{2,1,0:T(8,128)(2,1)S(1)}, u32[]{:S(2)}, u32[]{:S(2)}) %collective-permute-start.111) | collective-permute-done | bytes 360480 | tf_op jit(solution)/shard_map/ppermute | solution.py:179
  515.0 7.0 %collective-permute-done.112 = bf16[176,512]{1,0:T(8,128)(2,1)S(1)} collective-permute-done((bf16[176,512]{1,0:T(8,128)(2,1)S(1)}, bf16[176,512]{1,0:T(8,128)(2,1)S(1)}, u32[]{:S(2)}, u32[]{:S(2)}) %collective-permute-start.112) | collective-permute-done | bytes 180256 | tf_op jit(solution)/shard_map/ppermute | solution.py:179
  524.8 10.5 %collective-permute-done.113 = bf16[176,512]{1,0:T(8,128)(2,1)S(1)} collective-permute-done((bf16[176,512]{1,0:T(8,128)(2,1)S(1)}, bf16[176,512]{1,0:T(8,128)(2,1)S(1)}, u32[]{:S(2)}, u32[]{:S(2)}) %collective-permute-start.113) | collective-permute-done | bytes 180256 | tf_op jit(solution)/shard_map/ppermute | solution.py:179
  539.4 8.4 %collective-permute-done.114 = bf16[352,512]{1,0:T(8,128)(2,1)S(1)} collective-permute-done((bf16[352,512]{1,0:T(8,128)(2,1)S(1)}, bf16[352,512]{1,0:T(8,128)(2,1)S(1)}, u32[]{:S(2)}, u32[]{:S(2)}) %collective-permute-start.114) | collective-permute-done | bytes 360480 | tf_op jit(solution)/shard_map/ppermute | solution.py:179
  556.7 7.5 %collective-permute-done.115 = bf16[704,512]{1,0:T(8,128)(2,1)S(1)} collective-permute-done((bf16[704,512]{1,0:T(8,128)(2,1)S(1)}, bf16[704,512]{1,0:T(8,128)(2,1)S(1)}, u32[]{:S(2)}, u32[]{:S(2)}) %collective-permute-start.115) | collective-permute-done | bytes 720928 | tf_op jit(solution)/shard_map/ppermute | solution.py:179
  568.4 7.0 %collective-permute-done.67 = bf16[256,1024]{1,0:T(8,128)(2,1)S(1)} collective-permute-done((bf16[256,1024]{1,0:T(8,128)(2,1)S(1)}, bf16[256,1024]{1,0:T(8,128)(2,1)S(1)}, u32[]{:S(2)}, u32[]{:S(2)}) %collective-permute-start.67) | collective-permute-done | bytes 524320 | tf_op jit(solution)/shard_map/ppermute | solution.py:179
  (702 shorter events, 402.2 us)
Async XLA Ops:
  6.6 40.5 %collective-permute-start = (bf16[13696]{0:T(1024)(128)(2,1)S(1)}, bf16[13696]{0:T(1024)(128)(2,1)S(1)}, u32[]{:S(2)}, u32[]{:S(2)}) collective-permute-start(bf16[13696]{0:T(1024)(128)(2,1)S(1)} %dynamic-update-slice.17), channel_id=1, source_target_pairs={{0,16},{16,0},{1,17},{17,1},{2,18},{18,2},{3,19},{19,3},{4,20},{20... | collective-permute-start | bytes 82184 | tf_op jit(solution)/shard_map/ppermute | solution.py:178
  16.6 93.7 %collective-permute-start.1 = (bf16[128,3072]{1,0:T(8,128)(2,1)}, bf16[128,3072]{1,0:T(8,128)(2,1)}, u32[]{:S(2)}, u32[]{:S(2)}) collective-permute-start(bf16[128,3072]{1,0:T(8,128)(2,1)} %constant_dynamic-slice_fusion.26), channel_id=1, source_target_pairs={{0,16},{16,0},{1,17},{17,1},{2,18},{18,2},{3,19},{19,3},{4,20},{20... | collective-permute-start | bytes 2359304 | tf_op jit(solution)/shard_map/ppermute | solution.py:178
  18.3 34.7 %collective-permute-start.16 = (bf16[128,1024]{1,0:T(8,128)(2,1)}, bf16[128,1024]{1,0:T(8,128)(2,1)}, u32[]{:S(2)}, u32[]{:S(2)}) collective-permute-start(bf16[128,1024]{1,0:T(8,128)(2,1)} %constant_dynamic-slice_fusion.21), channel_id=1, source_target_pairs={{0,16},{16,0},{1,17},{17,1},{2,18},{18,2},{3,19},{19,3},{4,20},{20... | collective-permute-start | bytes 786440 | tf_op jit(solution)/shard_map/ppermute | solution.py:178
  21.4 45.3 %collective-permute-start.36 = (bf16[176,1024]{1,0:T(8,128)(2,1)}, bf16[176,1024]{1,0:T(8,128)(2,1)}, u32[]{:S(2)}, u32[]{:S(2)}) collective-permute-start(bf16[176,1024]{1,0:T(8,128)(2,1)} %constant_dynamic-slice_fusion.18), channel_id=1, source_target_pairs={{0,16},{16,0},{1,17},{17,1},{2,18},{18,2},{3,19},{19,3},{4,20},{20... | collective-permute-start | bytes 1081352 | tf_op jit(solution)/shard_map/ppermute | solution.py:178
  23.2 32.8 %collective-permute-start.28 = (bf16[64,2816]{1,0:T(8,128)(2,1)}, bf16[64,2816]{1,0:T(8,128)(2,1)}, u32[]{:S(2)}, u32[]{:S(2)}) collective-permute-start(bf16[64,2816]{1,0:T(8,128)(2,1)} %constant_dynamic-slice_fusion.19), channel_id=1, source_target_pairs={{0,16},{16,0},{1,17},{17,1},{2,18},{18,2},{3,19},{19,3},{4,20},{20... | collective-permute-start | bytes 1081352 | tf_op jit(solution)/shard_map/ppermute | solution.py:178
  66.7 275.0 %collective-permute-start.108 = (bf16[256,512]{1,0:T(8,128)(2,1)}, bf16[256,512]{1,0:T(8,128)(2,1)}, u32[]{:S(2)}, u32[]{:S(2)}) collective-permute-start(bf16[256,512]{1,0:T(8,128)(2,1)} %get-tuple-element.141), channel_id=1, source_target_pairs={{0,1},{1,0},{2,3},{3,2},{4,5},{5,4},{6,7},{7,6},{8,9},{9,8},{10,11... | collective-permute-start | bytes 786440 | tf_op jit(solution)/shard_map/ppermute | solution.py:179
  81.3 100.0 %collective-permute-start.40 = (bf16[176,1024]{1,0:T(8,128)(2,1)}, bf16[176,1024]{1,0:T(8,128)(2,1)S(1)}, u32[]{:S(2)}, u32[]{:S(2)}) collective-permute-start(bf16[176,1024]{1,0:T(8,128)(2,1)} %collective-permute-done.36), channel_id=1, source_target_pairs={{0,1},{1,0},{2,3},{3,2},{4,5},{5,4},{6,7},{7,6},{8,9},{9,8},{10,11... | collective-permute-start | bytes 1081352 | tf_op jit(solution)/shard_map/ppermute | solution.py:179
  98.0 30.3 %collective-permute-start.32 = (bf16[64,2816]{1,0:T(8,128)(2,1)}, bf16[64,2816]{1,0:T(8,128)(2,1)S(1)}, u32[]{:S(2)}, u32[]{:S(2)}) collective-permute-start(bf16[64,2816]{1,0:T(8,128)(2,1)} %collective-permute-done.28), channel_id=1, source_target_pairs={{0,1},{1,0},{2,3},{3,2},{4,5},{5,4},{6,7},{7,6},{8,9},{9,8},{10,11... | collective-permute-start | bytes 1081352 | tf_op jit(solution)/shard_map/ppermute | solution.py:179
  129.0 28.8 %collective-permute-start.33 = (bf16[64,2816]{1,0:T(8,128)(2,1)S(1)}, bf16[64,2816]{1,0:T(8,128)(2,1)S(1)}, u32[]{:S(2)}, u32[]{:S(2)}) collective-permute-start(bf16[64,2816]{1,0:T(8,128)(2,1)S(1)} %collective-permute-done.29), channel_id=1, source_target_pairs={{0,1},{1,0},{2,3},{3,2},{4,5},{5,4},{6,7},{7,6},{8,9},{9,8},{10,11... | collective-permute-start | bytes 1081352 | tf_op jit(solution)/shard_map/ppermute | solution.py:179
  182.1 100.5 %collective-permute-start.59 = (bf16[256,1024]{1,0:T(8,128)(2,1)}, bf16[256,1024]{1,0:T(8,128)(2,1)}, u32[]{:S(2)}, u32[]{:S(2)}) collective-permute-start(bf16[256,1024]{1,0:T(8,128)(2,1)} %fusion.63), channel_id=1, source_target_pairs={{0,1},{1,0},{2,3},{3,2},{4,5},{5,4},{6,7},{7,6},{8,9},{9,8},{10,11... | collective-permute-start | bytes 1572872 | tf_op jit(solution)/shard_map/ppermute | solution.py:179
  232.9 52.9 %collective-permute-start.78 = (bf16[256,1024]{1,0:T(8,128)(2,1)}, bf16[256,1024]{1,0:T(8,128)(2,1)}, u32[]{:S(2)}, u32[]{:S(2)}) collective-permute-start(bf16[256,1024]{1,0:T(8,128)(2,1)} %get-tuple-element.117), channel_id=1, source_target_pairs={{0,1},{1,0},{2,3},{3,2},{4,5},{5,4},{6,7},{7,6},{8,9},{9,8},{10,11... | collective-permute-start | bytes 1572872 | tf_op jit(solution)/shard_map/ppermute | solution.py:179
  285.9 57.4 %collective-permute-start.107 = (bf16[256,2816]{1,0:T(8,128)(2,1)S(1)}, bf16[256,2816]{1,0:T(8,128)(2,1)S(1)}, u32[]{:S(2)}, u32[]{:S(2)}) collective-permute-start(bf16[256,2816]{1,0:T(8,128)(2,1)S(1)} %copy-done.79), channel_id=1, source_target_pairs={{0,1},{1,0},{2,3},{3,2},{4,5},{5,4},{6,7},{7,6},{8,9},{9,8},{10,11... | collective-permute-start | bytes 4325384 | tf_op jit(solution)/shard_map/ppermute | solution.py:179
  322.3 62.5 %collective-permute-start.90 = (bf16[2,2,2,64,1408]{4,3,2,1,0:T(8,128)(2,1)S(1)}, bf16[2,2,2,64,1408]{4,3,2,1,0:T(8,128)(2,1)S(1)}, u32[]{:S(2)}, u32[]{:S(2)}) collective-permute-start(bf16[2,2,2,64,1408]{4,3,2,1,0:T(8,128)(2,1)S(1)} %dynamic-slice_bitcast_fusion.2), channel_id=1, source_target_pairs={{0,16},{16,0},{1,17},{17,1},{2,18},{18,2},{3,19},{19,3},{4,20},{20... | collective-permute-start | bytes 4325384 | tf_op jit(solution)/shard_map/ppermute | solution.py:178
  323.4 63.1 %collective-permute-start.99 = (bf16[2,2,2,64,1408]{4,3,2,1,0:T(8,128)(2,1)S(1)}, bf16[2,2,2,64,1408]{4,3,2,1,0:T(8,128)(2,1)S(1)}, u32[]{:S(2)}, u32[]{:S(2)}) collective-permute-start(bf16[2,2,2,64,1408]{4,3,2,1,0:T(8,128)(2,1)S(1)} %dynamic-slice_bitcast_fusion.1), channel_id=1, source_target_pairs={{0,16},{16,0},{1,17},{17,1},{2,18},{18,2},{3,19},{19,3},{4,20},{20... | collective-permute-start | bytes 4325384 | tf_op jit(solution)/shard_map/ppermute | solution.py:178
  350.4 96.0 %collective-permute-start.109 = (bf16[2,2,2,176,512]{4,3,2,1,0:T(8,128)(2,1)}, bf16[2,2,2,176,512]{4,3,2,1,0:T(8,128)(2,1)}, u32[]{:S(2)}, u32[]{:S(2)}) collective-permute-start(bf16[2,2,2,176,512]{4,3,2,1,0:T(8,128)(2,1)} %dynamic-slice_bitcast_fusion), channel_id=1, source_target_pairs={{0,16},{16,0},{1,17},{17,1},{2,18},{18,2},{3,19},{19,3},{4,20},{20... | collective-permute-start | bytes 4325384 | tf_op jit(solution)/shard_map/ppermute | solution.py:178
  384.8 44.7 %collective-permute-start.87 = (bf16[512,512]{1,0:T(8,128)(2,1)}, bf16[512,512]{1,0:T(8,128)(2,1)}, u32[]{:S(2)}, u32[]{:S(2)}) collective-permute-start(bf16[512,512]{1,0:T(8,128)(2,1)} %constant_dynamic-update-slice_fusion.18), channel_id=1, source_target_pairs={{0,1},{1,0},{2,3},{3,2},{4,5},{5,4},{6,7},{7,6},{8,9},{9,8},{10,11... | collective-permute-start | bytes 1572872 | tf_op jit(solution)/shard_map/ppermute | solution.py:179
  386.6 55.3 %collective-permute-start.91 = (bf16[2,2,64,1408]{3,2,1,0:T(8,128)(2,1)}, bf16[2,2,64,1408]{3,2,1,0:T(8,128)(2,1)}, u32[]{:S(2)}, u32[]{:S(2)}) collective-permute-start(bf16[2,2,64,1408]{3,2,1,0:T(8,128)(2,1)} %dynamic-slice_bitcast_fusion.6), channel_id=1, source_target_pairs={{0,2},{1,3},{2,0},{3,1},{4,6},{5,7},{6,4},{7,5},{8,10},{9,11},{10,... | collective-permute-start | bytes 2162696 | tf_op jit(solution)/shard_map/ppermute | solution.py:179
  389.2 54.3 %collective-permute-start.100 = (bf16[2,2,64,1408]{3,2,1,0:T(8,128)(2,1)}, bf16[2,2,64,1408]{3,2,1,0:T(8,128)(2,1)}, u32[]{:S(2)}, u32[]{:S(2)}) collective-permute-start(bf16[2,2,64,1408]{3,2,1,0:T(8,128)(2,1)} %dynamic-slice_bitcast_fusion.5), channel_id=1, source_target_pairs={{0,2},{1,3},{2,0},{3,1},{4,6},{5,7},{6,4},{7,5},{8,10},{9,11},{10,... | collective-permute-start | bytes 2162696 | tf_op jit(solution)/shard_map/ppermute | solution.py:179
  448.2 40.6 %collective-permute-start.110 = (bf16[2,2,176,512]{3,2,1,0:T(8,128)(2,1)S(1)}, bf16[2,2,176,512]{3,2,1,0:T(8,128)(2,1)S(1)}, u32[]{:S(2)}, u32[]{:S(2)}) collective-permute-start(bf16[2,2,176,512]{3,2,1,0:T(8,128)(2,1)S(1)} %dynamic-slice_bitcast_fusion.4), channel_id=1, source_target_pairs={{0,2},{1,3},{2,0},{3,1},{4,6},{5,7},{6,4},{7,5},{8,10},{9,11},{10,... | collective-permute-start | bytes 2162696 | tf_op jit(solution)/shard_map/ppermute | solution.py:179
  451.3 39.5 %collective-permute-start.61 = (bf16[2,2,2,64,1024]{4,3,2,1,0:T(8,128)(2,1)S(1)}, bf16[2,2,2,64,1024]{4,3,2,1,0:T(8,128)(2,1)S(1)}, u32[]{:S(2)}, u32[]{:S(2)}) collective-permute-start(bf16[2,2,2,64,1024]{4,3,2,1,0:T(8,128)(2,1)S(1)} %dynamic-slice_bitcast_fusion.3), channel_id=1, source_target_pairs={{0,16},{16,0},{1,17},{17,1},{2,18},{18,2},{3,19},{19,3},{4,20},{20... | collective-permute-start | bytes 3145736 | tf_op jit(solution)/shard_map/ppermute | solution.py:178
  495.7 42.6 %collective-permute-start.96 = (bf16[256,1408]{1,0:T(8,128)(2,1)S(1)}, bf16[256,1408]{1,0:T(8,128)(2,1)S(1)}, u32[]{:S(2)}, u32[]{:S(2)}) collective-permute-start(bf16[256,1408]{1,0:T(8,128)(2,1)S(1)} %constant_dynamic-update-slice_fusion.14), channel_id=1, source_target_pairs={{0,2},{1,3},{2,0},{3,1},{4,6},{5,7},{6,4},{7,5},{8,10},{9,11},{10,... | collective-permute-start | bytes 2162696 | tf_op jit(solution)/shard_map/ppermute | solution.py:179
  503.4 45.3 %collective-permute-start.105 = (bf16[256,1408]{1,0:T(8,128)(2,1)S(1)}, bf16[256,1408]{1,0:T(8,128)(2,1)S(1)}, u32[]{:S(2)}, u32[]{:S(2)}) collective-permute-start(bf16[256,1408]{1,0:T(8,128)(2,1)S(1)} %constant_dynamic-update-slice_fusion.8), channel_id=1, source_target_pairs={{0,2},{1,3},{2,0},{3,1},{4,6},{5,7},{6,4},{7,5},{8,10},{9,11},{10,... | collective-permute-start | bytes 2162696 | tf_op jit(solution)/shard_map/ppermute | solution.py:179
  538.4 39.4 %collective-permute-start.97 = (bf16[512,1408]{1,0:T(8,128)(2,1)S(1)}, bf16[512,1408]{1,0:T(8,128)(2,1)S(1)}, u32[]{:S(2)}, u32[]{:S(2)}) collective-permute-start(bf16[512,1408]{1,0:T(8,128)(2,1)S(1)} %constant_dynamic-update-slice_fusion.12), channel_id=1, source_target_pairs={{0,1},{1,0},{2,3},{3,2},{4,5},{5,4},{6,7},{7,6},{8,9},{9,8},{10,11... | collective-permute-start | bytes 4325384 | tf_op jit(solution)/shard_map/ppermute | solution.py:179
  548.8 29.3 %collective-permute-start.106 = (bf16[512,1408]{1,0:T(8,128)(2,1)S(1)}, bf16[512,1408]{1,0:T(8,128)(2,1)S(1)}, u32[]{:S(2)}, u32[]{:S(2)}) collective-permute-start(bf16[512,1408]{1,0:T(8,128)(2,1)S(1)} %constant_dynamic-update-slice_fusion.6), channel_id=1, source_target_pairs={{0,1},{1,0},{2,3},{3,2},{4,5},{5,4},{6,7},{7,6},{8,9},{9,8},{10,11... | collective-permute-start | bytes 4325384 | tf_op jit(solution)/shard_map/ppermute | solution.py:179
  (178 other events, 1634.9 us)

commit v2 on v1

v2 whole, which is shorter than its diff:
```python
import functools

import jax
import jax.numpy as jnp
from jax import lax
from jax.experimental import pallas as pl
from jax.experimental.pallas import tpu as pltpu
from jax.sharding import PartitionSpec as P

H = 4
DK = 128
DV = 256
SPAN = 64


epsilon = 1e-06
head_floor = 0.25
gate_scale = 16.0
highest = lax.Precision.HIGHEST
bf16 = jnp.bfloat16
f32 = jnp.float32


def rms_scale(values, scale_gain):
    return (
        values * lax.rsqrt(jnp.mean(values * values, axis=-1, keepdims=True) + epsilon) * scale_gain
    )


def mat_product(left, right):
    return jnp.dot(left, right, preferred_element_type=f32)


def cross_rows(left, right):
    return lax.dot_general(left, right, (((0,), (0,)), ((), ())), preferred_element_type=f32)


def back_product(left, right):
    return lax.dot_general(left, right, (((1,), (1,)), ((), ())), preferred_element_type=f32)


def dot(left, right, contract):
    return lax.dot_general(
        left, right, (((contract[0],), (contract[1],)), ((), ())), preferred_element_type=f32
    )


def fine(left, right, contract):
    lefts, rights = parts_of(left), parts_of(right)
    total = dot(lefts[0], rights[0], contract)
    if len(lefts) > 1:
        total = total + dot(lefts[1], rights[0], contract)
    if len(rights) > 1:
        total = total + dot(lefts[0], rights[1], contract)
    return total


def parts_of(array):
    if array.dtype == bf16:
        return (array,)
    high = array.astype(bf16)
    return high, (array - high.astype(f32)).astype(bf16)


def triangle():
    rows = lax.broadcasted_iota(jnp.int32, (SPAN, SPAN), 0)
    cols = lax.broadcasted_iota(jnp.int32, (SPAN, SPAN), 1)
    return rows >= cols


def block_terms(q_ref, k_ref, g_ref, head):
    cols = slice(head * DK, (head + 1) * DK)
    lower = jnp.where(triangle(), 1.0, 0.0).astype(bf16)
    c = jnp.dot(lower, g_ref[:, cols], preferred_element_type=f32)
    e = c[SPAN - 1 : SPAN, :]
    qt = q_ref[:, cols].astype(f32) * DK ** (-0.5) * jnp.exp(c)
    keys = k_ref[:, cols].astype(f32)
    return c, e, qt, keys * jnp.exp(-c), keys * jnp.exp(e - c)


def store_groups(ref, head, state):
    groups, size = ref.shape[1], ref.shape[2]
    count = state.shape[0] // groups
    for group in range(groups):
        ref[head, group, 0:count, :] = state[group * count : (group + 1) * count, :].astype(bf16)


def local_kernel(q_ref, k_ref, g_ref, v_ref, inside_ref, send_ref):
    groups = send_ref.shape[1]
    count = DV // groups
    place = lax.broadcasted_iota(jnp.int32, (16, DK), 0)
    for head in range(H):
        wide = slice(head * DV, (head + 1) * DV)
        c, e, qt, kt, kl = block_terms(q_ref, k_ref, g_ref, head)
        v = v_ref[:, wide]
        scores = jnp.where(triangle(), fine(qt, kt, (1, 1)), 0.0)
        inside_ref[:, wide] = fine(scores, v, (1, 0))
        store_groups(send_ref, head, fine(v, kl, (0, 0)))
        fade = jnp.exp(e)
        high = fade.astype(bf16).astype(f32)
        tail = jnp.where(place == 0, high, jnp.where(place == 1, fade - high, 0.0)).astype(bf16)
        for group in range(groups):
            send_ref[head, group, count : count + 16, :] = tail


def scan_kernel(backward, fade_ref, update_ref, before_ref):
    blocks, count, _ = before_ref.shape

    def step(i, state):
        block = blocks - 1 - i if backward else i
        before_ref[block] = state.astype(bf16)
        tail = fade_ref[block, count : count + 16, :].astype(f32)
        fade = tail[0:1, :] + tail[1:2, :]
        return state * fade + update_ref[block, 0:count, :].astype(f32)

    lax.fori_loop(0, blocks, step, jnp.zeros((count, DK), f32), unroll=4)


def scan_blocks(backward, received_fade, received):
    blocks, rows, _ = received_fade.shape
    return pl.pallas_call(
        functools.partial(scan_kernel, backward),
        out_shape=jax.ShapeDtypeStruct((blocks, rows - 16, DK), bf16),
        in_specs=[pl.BlockSpec(memory_space=pltpu.VMEM)] * 2,
        out_specs=pl.BlockSpec(memory_space=pltpu.VMEM),
        compiler_params=pltpu.CompilerParams(vmem_limit_bytes=24 * 1024 * 1024),
        cost_estimate=pl.CostEstimate(
            flops=4 * received.size, bytes_accessed=6 * received.size, transcendentals=0
        ),
    )(received_fade, received)


def outside_kernel(q_ref, k_ref, g_ref, inside_ref, state_ref, gate_ref, gain_ref, mixed_ref, gated_ref):
    for head in range(H):
        wide = slice(head * DV, (head + 1) * DV)
        c, e, qt, kt, kl = block_terms(q_ref, k_ref, g_ref, head)
        mixed = (inside_ref[:, wide] + fine(qt, state_ref[head], (1, 1))).astype(bf16)
        mixed_ref[:, wide] = mixed
        m = mixed.astype(f32)
        gate = gate_ref[:, wide]
        scale = lax.rsqrt(jnp.maximum(jnp.mean(m * m, axis=1, keepdims=True), head_floor))
        gated_ref[:, wide] = (m * scale * gain_ref[...] * (gate * jax.nn.sigmoid(gate))).astype(bf16)


def back_state_kernel(
    q_ref, k_ref, g_ref, dy_ref, mixed_ref, gate_ref, gain_ref,
    d_mixed_ref, d_gate_ref, gain_grad_ref, send_ref,
):
    gain_grad = jnp.zeros((1, DV), f32)
    gain = gain_ref[...]
    for head in range(H):
        wide = slice(head * DV, (head + 1) * DV)
        c, e, qt, kt, kl = block_terms(q_ref, k_ref, g_ref, head)
        m = mixed_ref[:, wide].astype(f32)
        gate = gate_ref[:, wide]
        dy = dy_ref[:, wide]
        square = jnp.mean(m * m, axis=1, keepdims=True)
        scale = lax.rsqrt(jnp.maximum(square, head_floor))
        sig = jax.nn.sigmoid(gate)
        silu = gate * sig
        unit = m * scale
        d_gate_ref[:, wide] = (dy * unit * gain * (sig * (1.0 + gate * (1.0 - sig)))).astype(bf16)
        d_normed = dy * silu
        gain_grad = gain_grad + jnp.sum(d_normed * unit, axis=0, keepdims=True)
        t = d_normed * gain
        inner = jnp.sum(t * m, axis=1, keepdims=True) * (1.0 / DV)
        share = jnp.where(square > head_floor, 1.0, jnp.where(square == head_floor, 0.5, 0.0))
        d_mixed = (t * scale - m * (inner * share * scale * scale * scale)).astype(bf16)
        d_mixed_ref[:, wide] = d_mixed
        store_groups(send_ref, head, fine(d_mixed, qt, (0, 0)))
    gain_grad_ref[0] = jnp.broadcast_to(gain_grad, (8, DV)) * 0.125


def back_kernel(
    q_ref, k_ref, g_ref, v_ref, do_ref, state_ref, after_ref, dq_ref, dk_ref, dg_ref, dv_ref
):
    mask = triangle()
    upper = jnp.where(
        lax.broadcasted_iota(jnp.int32, (SPAN, SPAN), 0)
        <= lax.broadcasted_iota(jnp.int32, (SPAN, SPAN), 1),
        1.0,
        0.0,
    ).astype(bf16)
    last = lax.broadcasted_iota(jnp.int32, (SPAN, DK), 0) == SPAN - 1
    for head in range(H):
        wide = slice(head * DV, (head + 1) * DV)
        cols = slice(head * DK, (head + 1) * DK)
        c, e, qt, kt, kl = block_terms(q_ref, k_ref, g_ref, head)
        v = v_ref[:, wide]
        do = do_ref[:, wide]
        state = state_ref[head]
        after = after_ref[head]
        scores = jnp.where(mask, fine(qt, kt, (1, 1)), 0.0)
        d_scores = jnp.where(mask, fine(do, v, (1, 1)), 0.0)
        dv_ref[:, wide] = (fine(scores, do, (0, 0)) + fine(kl, after, (1, 1))).astype(bf16)
        dqt = fine(d_scores, kt, (1, 0)) + fine(do, state, (1, 0))
        dkt = fine(d_scores, qt, (0, 0))
        dkl = fine(v, after, (1, 0))
        dq_ref[:, cols] = (dqt * (DK ** (-0.5) * jnp.exp(c))).astype(bf16)
        dk_ref[:, cols] = (dkt * jnp.exp(-c) + dkl * jnp.exp(e - c)).astype(bf16)
        tail = kl * dkl
        fade_grad = jnp.sum(after.astype(f32) * state.astype(f32), axis=0, keepdims=True)
        de = jnp.sum(tail, axis=0, keepdims=True) + jnp.exp(e) * fade_grad
        dc = qt * dqt - kt * dkt - tail + jnp.where(last, de, 0.0)
        dg_ref[:, cols] = fine(upper, dc, (1, 0)).astype(bf16)


def row_spec(width):
    return pl.BlockSpec((SPAN, width), lambda i: (i, 0))


def state_spec(groups, count):
    return pl.BlockSpec((H, groups, count, DK), lambda i: (i, 0, 0, 0))


def block_call(kernel, seq_count, in_specs, out_specs, out_shape, flops):
    return pl.pallas_call(
        kernel,
        grid=(seq_count,),
        in_specs=in_specs,
        out_specs=out_specs,
        out_shape=out_shape,
        compiler_params=pltpu.CompilerParams(vmem_limit_bytes=24 * 1024 * 1024),
        cost_estimate=pl.CostEstimate(
            flops=flops * seq_count * H, bytes_accessed=4 * 1024 * 1024, transcendentals=0
        ),
    )


class Links:
    def __init__(self):
        self.fsdp = lax.axis_index("fsdp")
        self.seq = lax.axis_index("seq")
        self.seq_count = lax.axis_size("seq")
        self.bits = self.seq_count.bit_length() - 1

    def own(self, axis):
        return self.fsdp if axis == "fsdp" else lax.rem(lax.div(self.seq, 1 << axis), 2)

    def swap_by_core(self, array, axes):
        if axes[0] == axes[1]:
            return self.swap(array, axes[0])
        count, moves = self.seq_count, []
        for fsdp in range(2):
            for seq in range(count):
                axis = axes[seq % 2]
                to = (1 - fsdp, seq) if axis == "fsdp" else (fsdp, seq ^ (1 << axis))
                moves.append((fsdp * count + seq, to[0] * count + to[1]))
        return lax.ppermute(array, ("fsdp", "seq"), moves)

    def by_core(self, pair):
        return jnp.where(self.own(0) == 0, pair[0], pair[1])

    def swap(self, array, axis):
        if axis == "fsdp":
            return lax.ppermute(array, "fsdp", [(0, 1), (1, 0)])
        return lax.ppermute(
            array, "seq", [(i, i ^ (1 << axis)) for i in range(self.seq_count)]
        )


def pick(array, index, axis=0):
    return lax.dynamic_index_in_dim(array, index, axis, keepdims=False)


def in_order(bit, own, other, axis):
    size = own.shape[axis]
    shape = list(own.shape)
    shape[axis] = 2 * size
    whole = jnp.zeros(shape, own.dtype)
    whole = lax.dynamic_update_slice_in_dim(whole, own, bit * size, axis)
    return lax.dynamic_update_slice_in_dim(whole, other, (1 - bit) * size, axis)


def own_piece(links, array, bit):
    rows = array.shape[0] // 4
    place = links.own(0) * 2 + links.own(bit)
    return lax.dynamic_slice_in_dim(array, place * rows, rows, 0)


def core_half(links, array):
    rows = array.shape[0] // 2
    return lax.dynamic_slice_in_dim(array, links.own(0) * rows, rows, 0)


def lay_down(links, *arrays):
    rows = arrays[0].shape[0]
    whole = jnp.zeros((2 * rows, sum(array.shape[1] for array in arrays)), bf16)
    col = 0
    for array in arrays:
        whole = lax.dynamic_update_slice(whole, array, (links.fsdp * rows, col))
        col += array.shape[1]
    return whole


def fill_other(links, whole, near, far):
    rows = whole.shape[0] // 2
    base = (1 - links.fsdp) * rows
    core = links.own(0)
    whole = lax.dynamic_update_slice(whole, near, (base + core * (rows // 2), 0))
    return lax.dynamic_update_slice(whole, far, (base + (1 - core) * (rows // 2), 0))


def feed_kernel(
    place_ref, norm_ref, dy_ref, gate_own, gate_near, gate_far, up_own, up_near, up_far, down_ref,
    hidden_ref, d_gate_ref, d_up_ref, final_ref, d_norm_ref,
):
    @pl.when(pl.program_id(0) == 0)
    def _():
        final_ref[...] = jnp.zeros_like(final_ref)
        d_norm_ref[...] = jnp.zeros_like(d_norm_ref)

    parts = []
    for i, (gate_part, up_part) in enumerate(
        ((gate_own, up_own), (gate_near, up_near), (gate_far, up_far))
    ):
        rows = gate_part.shape[0]
        parts.append((pl.ds(pl.multiple_of(place_ref[i], rows), rows), gate_part, up_part))
    gate = sum(dot(norm_ref[:, spot], part[...], (1, 0)) for spot, part, _ in parts)
    up = sum(dot(norm_ref[:, spot], part[...], (1, 0)) for spot, _, part in parts)
    down = down_ref[...]
    d_hidden = dot(dy_ref[...], down, (1, 1))
    sig = jax.nn.sigmoid(gate)
    silu = gate * sig
    hidden = (silu * up).astype(bf16)
    d_gate = (d_hidden * up * (sig * (1.0 + gate * (1.0 - sig)))).astype(bf16)
    d_up = (d_hidden * silu).astype(bf16)
    hidden_ref[...] = hidden
    d_gate_ref[...] = d_gate
    d_up_ref[...] = d_up
    final_ref[...] += dot(hidden, down, (1, 0))
    for spot, gate_part, up_part in parts:
        d_norm_ref[:, spot] += dot(d_gate, gate_part[...], (1, 1)) + dot(d_up, up_part[...], (1, 1))


def feed_forward(places, norm, dy, gates, ups, down):
    rows, width = norm.shape
    hidden_width = down.shape[0]
    block = 256
    still = lambda shape: pl.BlockSpec(shape, lambda j: (0, 0))
    along = lambda height: pl.BlockSpec((height, block), lambda j: (0, j))
    return pl.pallas_call(
        feed_kernel,
        grid=(hidden_width // block,),
        in_specs=[pl.BlockSpec(memory_space=pltpu.SMEM), still((rows, width)), still((rows, width))]
        + [along(part.shape[0]) for part in (*gates, *ups)]
        + [pl.BlockSpec((block, width), lambda j: (j, 0))],
        out_specs=[along(rows)] * 3 + [still((rows, width))] * 2,
        out_shape=[jax.ShapeDtypeStruct((rows, hidden_width), bf16)] * 3
        + [jax.ShapeDtypeStruct((rows, width), f32)] * 2,
        compiler_params=pltpu.CompilerParams(vmem_limit_bytes=36 * 1024 * 1024),
        cost_estimate=pl.CostEstimate(
            flops=12 * rows * width * hidden_width,
            bytes_accessed=6 * width * hidden_width,
            transcendentals=rows * hidden_width,
        ),
    )(places, norm, dy, *gates, *ups, down)


class Share:
    def __init__(self, links, partial, widths, halving, doubling):
        self.links, self.widths = links, widths
        groups, rows, self.cols = partial.shape
        self.rows = rows
        far = [("meet", (axis, axis)) for axis in range(3, links.bits)]
        self.steps = [("halve", axes) for axes in zip(*halving)] + far
        self.steps += [("double", axes) for axes in zip(*doubling)] + [("core", (0, 0))]
        self.left = (["fsdp", 1, 2], ["fsdp", 1, 2])
        self.data = partial.reshape((groups, 2, 2, 2, rows // 8, self.cols))
        self.outs = self.pending = None

    def cut(self, axes, other):
        links = self.links
        bits = [links.own(axis) for axis in axes]
        if other:
            bits = [1 - bit for bit in bits]
        dims = [1 + left.index(axis) for left, axis in zip(self.left, axes)]
        if dims[0] == dims[1]:
            return pick(self.data, bits[0] if axes[0] == axes[1] else links.by_core(bits), dims[0])
        return links.by_core([pick(self.data, bit, dim) for bit, dim in zip(bits, dims)])

    def receive(self, hold):
        if self.pending is None:
            return
        kind, axes, got = self.pending
        self.pending = None
        links, got = self.links, hold(got)
        if kind == "halve":
            kept = self.cut(axes, False)
            self.data = (kept.astype(f32) + got.astype(f32)).astype(bf16)
            for left, axis in zip(self.left, axes):
                left.remove(axis)
        elif kind == "meet":
            self.data = (self.data.astype(f32) + got.astype(f32)).astype(bf16)
        elif kind == "double":
            bits = [links.own(axis) for axis in axes]
            bit = bits[0] if axes[0] == axes[1] else links.by_core(bits)
            dims = [1 + sum(1 for o in left if o < axis) for left, axis in zip(self.left, axes)]
            data = in_order(bit, jnp.expand_dims(self.data, 1), jnp.expand_dims(got, 1), 1)
            moved = [jnp.moveaxis(data, 1, dim) for dim in dims]
            self.data = moved[0] if dims[0] == dims[1] else links.by_core(moved)
            for left, axis, dim in zip(self.left, axes, dims):
                left.insert(dim - 1, axis)
        else:
            shape = (self.data.shape[0], self.rows // 2, self.cols)
            own, other = self.data.reshape(shape), got.reshape(shape)
            self.outs = [
                out
                for i, widths in enumerate(self.widths)
                for out in finish_columns(self.links, own[i], other[i], widths)
            ]

    def step(self, after_last, hold):
        self.receive(after_last)
        kind, axes = self.steps.pop(0)
        send = self.cut(axes, True) if kind == "halve" else self.data
        got = self.links.swap_by_core(hold(send), axes)
        self.pending = (kind, axes, got)
        return got


def finish_kernel(widths, first_ref, own_ref, other_ref, *out_refs):
    first = first_ref[0] == 0
    low = jnp.where(first, own_ref[...], other_ref[...]).astype(f32)
    high = jnp.where(first, other_ref[...], own_ref[...]).astype(f32)
    offset = 0
    for width, out_ref in zip(widths, out_refs):
        half = width // 2
        out_ref[:, :half] = low[:, offset : offset + half]
        out_ref[:, half:] = high[:, offset : offset + half]
        offset += half


def finish_columns(links, own, other, widths):
    rows, cols = own.shape
    block = rows // 4
    spec = pl.BlockSpec((block, cols), lambda i: (i, 0))
    outs = pl.pallas_call(
        functools.partial(finish_kernel, widths),
        grid=(4,),
        in_specs=[pl.BlockSpec(memory_space=pltpu.SMEM), spec, spec],
        out_specs=[pl.BlockSpec((block, width), lambda i: (i, 0)) for width in widths],
        out_shape=[jax.ShapeDtypeStruct((rows, width), f32) for width in widths],
        compiler_params=pltpu.CompilerParams(vmem_limit_bytes=28 * 1024 * 1024),
        cost_estimate=pl.CostEstimate(flops=0, bytes_accessed=12 * own.size, transcendentals=0),
    )(links.own(0).reshape(1).astype(jnp.int32), own, other)
    return list(outs)


def half_columns(links, array, parts):
    mine = links.own(0)
    ours, theirs = [], []
    offset = 0
    for width in parts:
        piece = array[:, offset : offset + width]
        ours.append(lax.dynamic_slice_in_dim(piece, mine * (width // 2), width // 2, 1))
        theirs.append(lax.dynamic_slice_in_dim(piece, (1 - mine) * (width // 2), width // 2, 1))
        offset += width
    return join(ours), join(theirs)


def join(arrays):
    return arrays[0] if len(arrays) == 1 else jnp.concatenate(arrays, axis=1)


def with_other_core(links, ours, theirs):
    got = links.swap(join(theirs), 0)
    offset, outs = 0, []
    for array in ours:
        width = array.shape[1]
        outs.append(jnp.concatenate((array, got[:, offset : offset + width]), axis=0))
        offset += width
    return outs


def fence(*arrays):
    return lax.optimization_barrier(arrays)


def per_device(
    inputs,
    mixer_gain,
    query_weight,
    key_weight,
    value_weight,
    decay_down,
    decay_up,
    decay_bias,
    outgate_weight,
    head_gain,
    output_weight,
    feed_gain,
    feed_gate,
    feed_up,
    feed_down,
    cotangent,
):
    links = Links()
    seq_count, seg_rows, width = inputs.shape
    row_count = seq_count * seg_rows
    hidden_width = feed_gate.shape[1]
    key_cols, value_cols = H * DK, H * DV
    groups = links.seq_count // (seq_count * H)
    state_rows = DV // groups

    in_weights = (query_weight, key_weight, value_weight, outgate_weight)
    in_widths = (key_cols, key_cols, value_cols, value_cols)
    core = links.own(0)
    piece_in = join([core_half(links, weight) for weight in in_weights])
    near_in = links.swap(piece_in, "fsdp")
    piece_gate, piece_up = own_piece(links, feed_gate, 1), core_half(links, feed_up)
    piece_out = jnp.concatenate(
        (own_piece(links, feed_down, 1), own_piece(links, output_weight, 1)), axis=0
    )
    out_rows = (feed_down.shape[0] // 4, output_weight.shape[0] // 4)
    mine1 = links.own(1)
    full_in = lay_down(links, *in_weights)

    small = (mixer_gain, decay_down, decay_up, decay_bias, head_gain, feed_gain)
    packed = jnp.concatenate([piece.reshape(-1) for piece in small])
    packed_other = links.swap(packed, "fsdp")

    far_in = links.swap(near_in, 0)
    y_out = links.swap(fence(piece_out, near_in, full_in)[0], "fsdp")
    full_in = fill_other(links, full_in, near_in, far_in)

    low_half = jnp.where(links.fsdp == 0, packed, packed_other)
    high_half = jnp.where(links.fsdp == 0, packed_other, packed)
    whole_small = []
    offset = 0
    for piece in small:
        parts = [half[offset : offset + piece.size].reshape(piece.shape) for half in (low_half, high_half)]
        whole_small.append(jnp.concatenate(parts, axis=0))
        offset += piece.size
    full_mixer_gain, full_down, full_up_rank, full_bias, full_head_gain, full_feed_gain = whole_small
    head_gain_row = full_head_gain.astype(f32).reshape(1, DV)

    residual_in = inputs.reshape(row_count, width).astype(f32)
    normed_full, first_pull = jax.vjp(rms_scale, residual_in, full_mixer_gain.astype(f32))
    normed = normed_full.astype(bf16)
    projected = mat_product(normed, full_in)
    query = projected[:, :key_cols].astype(bf16)
    keys = projected[:, key_cols : 2 * key_cols].astype(bf16)
    values = projected[:, 2 * key_cols : 2 * key_cols + value_cols].astype(bf16)
    out_gate = projected[:, 2 * key_cols + value_cols :]
    ranked = mat_product(normed, full_down).astype(bf16)
    decay_in = mat_product(ranked, full_up_rank) + full_bias.astype(f32)
    decay = (jax.nn.log_sigmoid(decay_in) / gate_scale).astype(bf16)

    qkg_specs = [row_spec(key_cols)] * 3
    rows_wide = row_spec(value_cols)
    gain_spec = pl.BlockSpec((1, DV), lambda i: (0, 0))
    whole_state = pl.BlockSpec((H, DV, DK), lambda i: (i, 0, 0))
    wide_shape = jax.ShapeDtypeStruct((row_count, value_cols), bf16)
    block_flops = 2 * SPAN * DK * DV * 6

    def to_heads(array):
        rows = array.shape[2]
        return lax.all_to_all(
            array.reshape(links.seq_count, rows, DK), "seq", split_axis=0, concat_axis=0, tiled=True
        )

    def to_tokens(array):
        back = lax.all_to_all(array, "seq", split_axis=0, concat_axis=0, tiled=True)
        return back.reshape(seq_count * H, DV, DK)

    inside, update = block_call(
        local_kernel,
        seq_count,
        qkg_specs + [rows_wide],
        [rows_wide, state_spec(groups, state_rows + 16)],
        [
            jax.ShapeDtypeStruct((row_count, value_cols), f32),
            jax.ShapeDtypeStruct((seq_count * H, groups, state_rows + 16, DK), bf16),
        ],
        2 * block_flops,
    )(query, keys, decay, values)
    y_gate = links.swap(fence(piece_gate, y_out, update)[0], "fsdp")
    near_up = links.swap(fence(piece_up, y_gate)[0], "fsdp")
    y_out = fence(y_out, update)[0]
    x_out = links.swap(y_out, 1)
    x_gate = links.swap(y_gate, 1)
    received = to_heads(update)
    before = scan_blocks(False, received, received)
    near_up, x_gate = fence(near_up, before)[0], fence(x_gate, before)[0]
    full_feed_down = lay_down(links, fence(feed_down, update)[0])
    full_output = lay_down(links, fence(output_weight, update)[0])
    near_down = in_order(mine1, y_out[: out_rows[0]], x_out[: out_rows[0]], 0)
    near_output = in_order(mine1, y_out[out_rows[0] :], x_out[out_rows[0] :], 0)
    far_out = links.swap(jnp.concatenate((near_down, near_output), axis=0), 0)
    far_down, far_output = far_out[: 2 * out_rows[0]], far_out[2 * out_rows[0] :]
    full_feed_down = fill_other(links, full_feed_down, near_down, far_down)
    full_output = fill_other(links, full_output, near_output, far_output)
    near_gate = in_order(mine1, y_gate, x_gate, 0)
    far_gate = links.swap(near_gate, 0)
    far_up = links.swap(near_up, 0)
    d_down = cotangent.reshape(row_count, width)
    seq_grad = d_down.astype(f32)
    down_ours, down_theirs = half_columns(links, d_down, (width,))
    normed_both, down_both = with_other_core(
        links, (normed, down_ours), (fence(normed, update)[0], down_theirs)
    )
    state = to_tokens(before)
    mixed, gated = block_call(
        outside_kernel,
        seq_count,
        qkg_specs + [rows_wide, whole_state, rows_wide, gain_spec],
        [rows_wide] * 2,
        [wide_shape] * 2,
        block_flops,
    )(query, keys, decay, inside, state, out_gate, head_gain_row)


    middle = residual_in + mat_product(gated, full_output)
    second_full, second_pull = jax.vjp(rms_scale, middle, full_feed_gain.astype(f32))
    second_norm = second_full.astype(bf16)
    half = width // 2
    other_base = (1 - links.fsdp) * half
    places = jnp.stack(
        (links.fsdp * half, other_base + core * (half // 2), other_base + (1 - core) * (half // 2))
    ).astype(jnp.int32)
    hidden, d_gate, d_up, fed, d_second = feed_forward(
        places,
        second_norm,
        d_down,
        (feed_gate, near_gate, far_gate),
        (feed_up, near_up, far_up),
        full_feed_down,
    )
    output = (middle + fed).astype(bf16).reshape(seq_count, seg_rows, width)

    (second_both,) = with_other_core(links, (second_norm,), (second_norm,))
    (hidden_both,) = with_other_core(links, (hidden,), (hidden,))
    grad_down = cross_rows(hidden_both, down_both).astype(bf16)

    x, y, z = 1, "fsdp", 2
    cuts = (([y, x, z], [x, z, y]), ([y, z, x], [z, x, y]), ([y, x, z], [y, z, x]))
    joins = ([z, x], [x, z])
    shares, arrived, sent, extras = {}, [], [], []

    def after_last(array):
        return fence(array, *sent[-1:])[0]

    def hold(array, *due):
        behind = (*arrived[-4:-3], *sent[-1:], *extras, *due)
        sent.append(array)
        return fence(array, *behind)[0]

    def go(*names):
        for name in names:
            share = shares[name]
            if not share.steps:
                share.receive(after_last)
                sent.append(share.outs[0])
                continue
            arrived.append(share.step(after_last, hold))
            while share.steps and share.steps[0][0] == "meet" and share.steps[0][1][0] > 3:
                arrived.append(share.step(after_last, hold))

    shares["down"] = Share(links, grad_down[None], [(width,)], cuts[0], joins)
    go("down")
    d_second = fence(d_second, sent[0])[0]

    gate_ours, gate_theirs = half_columns(links, d_gate, (hidden_width,))
    up_ours, up_theirs = half_columns(links, d_up, (hidden_width,))
    gate_both, up_both = with_other_core(links, (gate_ours, up_ours), (gate_theirs, up_theirs))
    grad_gate = cross_rows(second_both, gate_both).astype(bf16)
    grad_up = cross_rows(second_both, up_both).astype(bf16)

    d_middle_norm, grad_feed_gain = second_pull(d_second)
    d_middle = seq_grad + d_middle_norm
    d_branch = d_middle.astype(bf16)
    d_gated = back_product(d_branch, full_output)
    d_mixed, d_outgate, gain_parts, back_update = block_call(
        back_state_kernel,
        seq_count,
        qkg_specs + [rows_wide] * 3 + [gain_spec],
        [rows_wide] * 2
        + [pl.BlockSpec((1, 8, DV), lambda i: (i, 0, 0)), state_spec(groups, state_rows)],
        [wide_shape] * 2
        + [
            jax.ShapeDtypeStruct((seq_count, 8, DV), f32),
            jax.ShapeDtypeStruct((seq_count * H, groups, state_rows, DK), bf16),
        ],
        block_flops,
    )(query, keys, decay, d_gated, mixed, out_gate, head_gain_row)
    grad_head_gain = jnp.sum(gain_parts, axis=(0, 1))
    branch_ours, branch_theirs = half_columns(links, d_branch, (width,))
    outgate_ours, outgate_theirs = half_columns(links, d_outgate, (value_cols,))
    gated_both, branch_both, outgate_both = with_other_core(
        links, (gated, branch_ours, outgate_ours), (gated, branch_theirs, outgate_theirs)
    )
    grad_mixer_out = fence(
        jnp.stack(
            (
                cross_rows(gated_both, branch_both).astype(bf16),
                cross_rows(normed_both, outgate_both).astype(bf16),
            )
        )
    )[0]

    back_received = to_heads(hold(back_update))
    shares["gate"] = Share(links, grad_gate[None], [(hidden_width,)], cuts[1], joins)
    shares["out"] = Share(links, grad_mixer_out, [(width,), (value_cols,)], cuts[0], joins)
    shares["up"] = Share(links, grad_up[None], [(hidden_width,)], cuts[2], joins)
    go("gate", "out", "down")
    after = to_tokens(hold(scan_blocks(True, received, after_last(back_received))))
    go("up", "gate", "down")
    after = after_last(after)
    d_query, d_keys, d_decay, d_values = block_call(
        back_kernel,
        seq_count,
        qkg_specs + [rows_wide] * 2 + [whole_state] * 2,
        [row_spec(key_cols)] * 3 + [rows_wide],
        [jax.ShapeDtypeStruct((row_count, key_cols), bf16)] * 3 + [wide_shape],
        4 * block_flops,
    )(query, keys, decay, values, d_mixed, state, after)
    d_qkv = jnp.concatenate((d_query, d_keys, d_values), axis=1)
    qkv_ours, qkv_theirs = half_columns(links, d_qkv, in_widths[:3])
    (qkv_both,) = with_other_core(links, (qkv_ours,), (qkv_theirs,))
    grad_qkv = cross_rows(normed_both, qkv_both).astype(bf16)
    shares["qkv"] = Share(links, grad_qkv[None], [in_widths[:3]], cuts[1], joins)
    sent.append(d_query)
    go("qkv")
    d_qkv, d_decay, _ = fence(d_qkv, d_decay, sent[-1])

    d_decay_in = d_decay.astype(f32) * jax.nn.sigmoid(-decay_in) / gate_scale
    grad_decay_bias = jnp.sum(d_decay_in, axis=0)
    grad_decay_up = lax.dot_general(
        ranked.astype(f32), d_decay_in, (((0,), (0,)), ((), ())), precision=highest
    )
    d_ranked = lax.dot_general(
        d_decay_in, full_up_rank.astype(f32), (((1,), (1,)), ((), ())), precision=highest
    ).astype(bf16)
    grad_decay_down = cross_rows(normed, d_ranked)
    d_normed = back_product(
        jnp.concatenate((d_qkv, d_outgate), axis=1), full_in
    ) + back_product(d_ranked, full_down)
    d_input_norm, grad_mixer_gain = first_pull(d_normed)
    input_grad = (d_middle + d_input_norm).reshape(seq_count, seg_rows, width)

    small_grads = (
        grad_mixer_gain, grad_decay_down, grad_decay_up, grad_decay_bias, grad_head_gain,
        grad_feed_gain,
    )
    total = jnp.concatenate([grad.reshape(2, -1) for grad in small_grads], axis=1)
    go("up", "gate", "down", "out")
    other = links.swap(hold(pick(total, 1 - links.fsdp), input_grad, output), "fsdp")
    go("up", "qkv", "gate")
    total = (pick(total, links.fsdp) + after_last(other)).reshape(links.seq_count, -1)
    pieces = lax.all_to_all(hold(total), "seq", split_axis=0, concat_axis=0, tiled=True)
    go("out", "qkv", "up", "gate")
    own_sum = jnp.sum(after_last(pieces), axis=0, keepdims=True)
    own_sum = hold(jnp.broadcast_to(own_sum, total.shape))
    total = lax.all_to_all(own_sum, "seq", split_axis=0, concat_axis=0, tiled=True)
    go("down", "out", "up", "down", "qkv", "gate")
    total = after_last(total).reshape(-1)
    small_out = []
    offset = 0
    for grad in small_grads:
        size = grad.size // 2
        small_out.append(
            total[offset : offset + size].reshape((grad.shape[0] // 2,) + grad.shape[1:])
        )
        offset += size
    out_mixer_gain, out_decay_down, out_decay_up, out_bias, out_head_gain, out_feed_gain = small_out
    extras.extend(small_out)
    go("qkv", "out", "up", "down", "qkv", "down", "out", "gate", "qkv", "up", "gate", "out", "qkv", "up", "out")
    results = [
        out for name in ("down", "gate", "up", "out", "qkv") for out in shares[name].outs
    ]


    (
        out_down, out_gate_w, out_up_w, out_output, out_outgate, out_query, out_key, out_value,
    ) = results
    return (
        output,
        input_grad,
        out_mixer_gain,
        out_query,
        out_key,
        out_value,
        out_decay_down,
        out_decay_up,
        out_bias,
        out_outgate,
        out_head_gain,
        out_output,
        out_feed_gain,
        out_gate_w,
        out_up_w,
        out_down,
    )


def solution(mesh):
    rows = P("fsdp", None)
    gains = P("fsdp")
    tokens = P("fsdp", "seq", None)
    weights = (gains, rows, rows, rows, rows, rows, gains, rows, gains, rows, gains, rows, rows, rows)
    return jax.shard_map(
        per_device,
        mesh=mesh,
        in_specs=(tokens,) + weights + (tokens,),
        out_specs=(tokens, tokens) + weights,
        check_vma=False,
    )
```

time: 602 us -> 494 us (0.82)
  waiting for transfers between devices: 211 us -> 138 us
  starting transfers between devices: 137 us -> 96.5 us
  matrix products: 59.1 us -> 30.4 us
  Pallas kernels: 29.8 us -> 54.9 us
  local copies, waits for them, and re-layouts: 99.5 us -> 113 us
    ppermute x94 -> x22, waiting for transfers between devices: 189 us -> 33.4 us  [swap(): lax.ppermute(array, 'seq', [(i, i ^ 1 << axis) for i in range(self.seq_co...]
    ppermute x94 -> x22, starting transfers between devices: 105 us -> 27.8 us  [swap(): lax.ppermute(array, 'seq', [(i, i ^ 1 << axis) for i in range(self.seq_co...]
    ppermute x10 -> x24, waiting for transfers between devices: 7.9 us -> 67.7 us  [swap_by_core(): return lax.ppermute(array, ('fsdp', 'seq'), moves)]
    all_to_all x0 -> x6, starting transfers between devices: none -> 34.3 us  [the longest x2 12.9 us: to_tokens(): back = lax.all_to_all(array, 'seq', split_axis=0, concat_axis=0, tiled=True)]
    pallas_call x4 -> x13, Pallas kernels: 29.8 us -> 54.9 us  [the longest x6 16.2 us: finish_columns(): pl.pallas_call(functools.partial(finish_kernel, widths), grid=(4,), in_sp...]
    dynamic_update_slice x37 -> x12, local copies, waits for them, and re-layouts: 34.2 us -> 15 us  [the longest x6 6.08 us: lay_down(): whole = lax.dynamic_update_slice(whole, array, (links.fsdp * rows, col))]
    dot_general x7 -> x4, matrix products: 26.1 us -> 8.6 us  [mat_product(): return jnp.dot(left, right, preferred_element_type=f32)]
    ppermute x13 -> x7, waiting for transfers between devices: 14 us -> 28.9 us  [swap(): return lax.ppermute(array, 'fsdp', [(0, 1), (1, 0)])]
  transfers between devices with their start and end apart: 117 -> 59, of which waited for: 49 -> 20; matrix products, arithmetic and copies ran while one was open for 33% -> 32% of each run, Pallas kernels for 5% -> 11%
where the time goes in v2:
time: 494 us; the launch traced here: 484 us
  waiting for transfers between devices  138 us (28%)
  local copies, waits for them, and re-layouts  113 us (23%)
  starting transfers between devices  96.5 us (20%)
  Pallas kernels  54.9 us (11%)
  other arithmetic  48.6 us (10%)
  matrix products  30.4 us (6%)
    ppermute x24, waiting for transfers between devices, swap_by_core(): return lax.ppermute(array, ('fsdp', 'seq'), moves)  67.7 us
    ppermute x22, waiting for transfers between devices, swap(): lax.ppermute(array, 'seq', [(i, i ^ 1 << axis) for i in range(self.seq_co...  33.4 us
    unnamed x266, local copies, waits for them, and re-layouts  29 us
    ppermute x7, waiting for transfers between devices, swap(): return lax.ppermute(array, 'fsdp', [(0, 1), (1, 0)])  28.9 us
    ppermute x22, starting transfers between devices, swap(): lax.ppermute(array, 'seq', [(i, i ^ 1 << axis) for i in range(self.seq_co...  27.8 us
    ppermute x24, starting transfers between devices, swap_by_core(): return lax.ppermute(array, ('fsdp', 'seq'), moves)  23.6 us
    convert_element_type x15, other arithmetic, receive(): self.data = (kept.astype(f32) + got.astype(f32)).astype(bf16)  18.3 us
    pallas_call x6, Pallas kernels, finish_columns(): pl.pallas_call(functools.partial(finish_kernel, widths), grid=(4,), in_sp...  16.2 us
  transfers between devices with their start and end apart: 59, of which 20 were waited for; matrix products, arithmetic and copies ran while one was open for 32% of the time, Pallas kernels for 11%

profile of v2, /device:TPU:1, one launch (start us, length us, event | category | flops | bytes accessed | tf_op | source)
XLA Modules:
  0.0 484.3 jit_solution(3846891883785449327)
XLA Ops:
  20.1 20.6 %collective-permute-done = bf16[13696]{0:T(1024)(128)(2,1)S(1)} collective-permute-done((bf16[13696]{0:T(1024)(128)(2,1)S(1)}, bf16[13696]{0:T(1024)(128)(2,1)S(1)}, u32[]{:S(2)}, u32[]{:S(2)}) %collective-permute-start) | collective-permute-done | bytes 27424 | tf_op jit(solution)/shard_map/ppermute | solution.py:256
  50.3 6.2 %fusion.77 = (bf16[256,3072]{1,0:T(8,128)(2,1)S(1)}, f32[256,3072]{1,0:T(8,128)}) fusion(bf16[256,1024]{1,0:T(8,128)(2,1)S(1)} %fusion.36, bf16[1024,3072]{1,0:T(8,128)(2,1)} %constant_dynamic-update-slice_fusion.6), kind=kOutput, calls=%fused_computation.256 | convolution fusion | flops 1611399168 | bytes 11534336 | tf_op jit(solution)/shard_map/dot_general | solution.py:31
  56.7 5.9 %shard_map.279 = (f32[256,1024]{1,0:T(8,128)S(1)}, bf16[16,1,272,128]{3,2,1,0:T(8,128)(2,1)}) custom-call(bf16[256,512]{1,0:T(8,128)(2,1)S(1)} %get-tuple-element.297.q_ref, bf16[256,512]{1,0:T(8,128)(2,1)S(1)} %get-tuple-element.296.k_ref, bf16[256,512]{1,0:T(8,128)(2,1)S(1)} %get-tuple-element.338.g_ref, bf16[256,1024]{1,0:T(8,128)(2,1)S(1)} %slice.199.v_ref), custom_call_target="tpu_custom_call" | custom-call | flops 805306368 | bytes 4194304 | tf_op jit(solution)/shard_map/pallas_call | solution.py:567
  63.6 4.9 %collective-permute-done.3 = bf16[480,1024]{1,0:T(8,128)(2,1)} collective-permute-done((bf16[480,1024]{1,0:T(8,128)(2,1)}, bf16[480,1024]{1,0:T(8,128)(2,1)}, u32[]{:S(2)}, u32[]{:S(2)}) %collective-permute-start.3) | collective-permute-done | bytes 983072 | tf_op jit(solution)/shard_map/ppermute | solution.py:256
  72.0 6.0 %all-to-all-start = ((bf16[16,272,128]{2,1,0:T(8,128)(2,1)}), bf16[16,272,128]{2,1,0:T(8,128)(2,1)S(1)}, u32[]{:S(2)}, u32[]{:S(2)}) async-start(bf16[16,272,128]{2,1,0:T(8,128)(2,1)} %bitcast.1), calls=%async_computation | async-start | bytes 2228224 | tf_op jit(solution)/shard_map/all_to_all | solution.py:559
  82.4 15.6 %collective-permute-done.4 = bf16[480,1024]{1,0:T(8,128)(2,1)} collective-permute-done((bf16[480,1024]{1,0:T(8,128)(2,1)}, bf16[480,1024]{1,0:T(8,128)(2,1)}, u32[]{:S(2)}, u32[]{:S(2)}) %collective-permute-start.4) | collective-permute-done | bytes 983072 | tf_op jit(solution)/shard_map/ppermute | solution.py:257
  101.8 5.2 %collective-permute-start.5 = (bf16[960,1024]{1,0:T(8,128)(2,1)}, bf16[960,1024]{1,0:T(8,128)(2,1)}, u32[]{:S(2)}, u32[]{:S(2)}) collective-permute-start(bf16[960,1024]{1,0:T(8,128)(2,1)} %pad_maximum_fusion.1), channel_id=1, source_target_pairs={{0,1},{1,0},{2,3},{3,2},{4,5},{5,4},{6,7},{7,6},{8,9},{9,8},{10,11... | collective-permute-start | bytes 5898248 | tf_op jit(solution)/shard_map/ppermute | solution.py:257
  112.9 5.8 %all-to-all-start.1 = ((bf16[16,256,128]{2,1,0:T(8,128)(2,1)}), bf16[16,256,128]{2,1,0:T(8,128)(2,1)S(1)}, u32[]{:S(2)}, u32[]{:S(2)}) async-start(bf16[16,256,128]{2,1,0:T(8,128)(2,1)} %shard_map.280), calls=%async_computation.1 | async-start | bytes 2097152 | tf_op jit(solution)/shard_map/all_to_all | solution.py:564
  130.0 4.0 collective-permute-done.7
  156.0 15.8 %shard_map.282 = (bf16[256,2816]{1,0:T(8,128)(2,1)}, bf16[256,2816]{1,0:T(8,128)(2,1)S(1)}, bf16[256,2816]{1,0:T(8,128)(2,1)S(1)}, f32[256,1024]{1,0:T(8,128)S(1)}, f32[256,1024]{1,0:T(8,128)S(1)}) custom-call(s32[3]{0:T(128)S(1)} %pad_add_fusion.place_ref, bf16[256,1024]{1,0:T(8,128)(2,1)S(1)} %multiply_convert_fusion.norm_ref, ...), custom_call_target="tpu_custom_call" | custom-call | flops 8858370048 | bytes 17301504 | tf_op jit(solution)/shard_map/pallas_call | solution.py:342
  198.4 5.7 %all-to-all-start.2 = ((bf16[16,256,128]{2,1,0:T(8,128)(2,1)}), bf16[16,256,128]{2,1,0:T(8,128)(2,1)S(1)}, u32[]{:S(2)}, u32[]{:S(2)}) async-start(bf16[16,256,128]{2,1,0:T(8,128)(2,1)} %bitcast.264), calls=%async_computation.2 | async-start | bytes 2097152 | tf_op jit(solution)/shard_map/all_to_all | solution.py:559
  228.5 7.1 %all-to-all-start.3 = ((bf16[16,256,128]{2,1,0:T(8,128)(2,1)}), bf16[16,256,128]{2,1,0:T(8,128)(2,1)}, u32[]{:S(2)}, u32[]{:S(2)}) async-start(bf16[16,256,128]{2,1,0:T(8,128)(2,1)} %copy-done.6), calls=%async_computation.3 | async-start | bytes 2097152 | tf_op jit(solution)/shard_map/all_to_all | solution.py:564
  248.0 16.0 %collective-permute-done.15 = bf16[1,2,352,512]{3,2,1,0:T(8,128)(2,1)S(1)} collective-permute-done((bf16[1,2,352,512]{3,2,1,0:T(8,128)(2,1)S(1)}, bf16[1,2,352,512]{3,2,1,0:T(8,128)(2,1)S(1)}, u32[]{:S(2)}, u32[]{:S(2)}) %collective-permute-start.15) | collective-permute-done | bytes 720928 | tf_op jit(solution)/shard_map/ppermute | solution.py:249
  268.0 10.3 %shard_map.285 = (bf16[256,512]{1,0:T(8,128)(2,1)S(1)}, bf16[256,512]{1,0:T(8,128)(2,1)S(1)}, bf16[256,512]{1,0:T(8,128)(2,1)S(1)}, bf16[256,1024]{1,0:T(8,128)(2,1)S(1)}) custom-call(bf16[256,512]{1,0:T(8,128)(2,1)S(1)} %copy-done.10, bf16[256,512]{1,0:T(8,128)(2,1)S(1)} %get-tuple-element.296.k_ref, bf16[256,512]{1,0:T(8,128)(2,1)S(1)} %copy-done.23, ...), custom_call_target="tpu_custom_call" | custom-call | flops 1610612736 | bytes 4194304 | tf_op jit(solution)/shard_map/pallas_call | solution.py:710
  309.0 5.8 %fusion.37 = (f32[1024]{0:T(1024)S(1)}, f32[256]{0:T(256)S(1)}, f32[256,1024]{1,0:T(8,128)}) fusion(bf16[4,64,1024]{2,1,0:T(8,128)(2,1)S(1)} %copy-done.62, f32[256]{0:T(256)S(1)} %copy-done.116, f32[1024]{0:T(1024)S(1)} %maximum_convert_fusion, f32[256,1024]{1,0:T(8,128)S(1)} %fusion.56, bf16[1024,3072]{1,0:T(8,128)(2,1)} %constant_dynamic-update-slice_fusion.6, ...), kind=kOutput, calls=%fused_computation.84 | convolution fusion | flops 1615854336 | bytes 10496000 | tf_op jit(solution)/shard_map/dot_general | solution.py:39
  323.0 20.6 %collective-permute-done.21 = bf16[1,2,128,1408]{3,2,1,0:T(8,128)(2,1)} collective-permute-done((bf16[1,2,128,1408]{3,2,1,0:T(8,128)(2,1)}, bf16[1,2,128,1408]{3,2,1,0:T(8,128)(2,1)}, u32[]{:S(2)}, u32[]{:S(2)}) %collective-permute-start.21) | collective-permute-done | bytes 720928 | tf_op jit(solution)/shard_map/ppermute | solution.py:249
  367.0 4.0 all-to-all-start.4
  383.7 5.8 %all-to-all-start.5 = ((f32[16,1,856]{2,1,0:T(1,128)}), f32[16,1,856]{2,1,0:T(1,128)S(1)}, u32[]{:S(2)}, u32[]{:S(2)}) async-start(f32[16,1,856]{2,1,0:T(1,128)} %all_to_all.35), calls=%async_computation.5 | async-start | bytes 114688 | tf_op jit(solution)/shard_map/all_to_all | solution.py:755
  396.9 8.2 %all-to-all-done.5 = f32[16,1,856]{2,1,0:T(1,128)S(1)} async-done(((f32[16,1,856]{2,1,0:T(1,128)}), f32[16,1,856]{2,1,0:T(1,128)S(1)}, u32[]{:S(2)}, u32[]{:S(2)}) %all-to-all-start.5) | async-done | bytes 54816 | tf_op jit(solution)/shard_map/all_to_all | solution.py:755
  415.0 6.5 %collective-permute-done.38 = bf16[1,128,1024]{2,1,0:T(8,128)(2,1)} collective-permute-done((bf16[1,128,1024]{2,1,0:T(8,128)(2,1)S(1)}, bf16[1,128,1024]{2,1,0:T(8,128)(2,1)}, u32[]{:S(2)}, u32[]{:S(2)}) %collective-permute-start.38) | collective-permute-done | bytes 262176 | tf_op jit(solution)/shard_map/ppermute | solution.py:257
  424.8 11.4 %collective-permute-done.41 = bf16[1,2,352,512]{3,2,1,0:T(8,128)(2,1)S(1)} collective-permute-done((bf16[1,2,352,512]{3,2,1,0:T(8,128)(2,1)S(1)}, bf16[1,2,352,512]{3,2,1,0:T(8,128)(2,1)S(1)}, u32[]{:S(2)}, u32[]{:S(2)}) %collective-permute-start.41) | collective-permute-done | bytes 720928 | tf_op jit(solution)/shard_map/ppermute | solution.py:249
  437.9 6.4 %collective-permute-done.40 = bf16[1,128,1024]{2,1,0:T(8,128)(2,1)S(1)} collective-permute-done((bf16[1,128,1024]{2,1,0:T(8,128)(2,1)S(1)}, bf16[1,128,1024]{2,1,0:T(8,128)(2,1)S(1)}, u32[]{:S(2)}, u32[]{:S(2)}) %collective-permute-start.40) | collective-permute-done | bytes 262176 | tf_op jit(solution)/shard_map/ppermute | solution.py:249
  453.0 5.5 %collective-permute-done.43 = bf16[1,2,128,1024]{3,2,1,0:T(8,128)(2,1)S(1)} collective-permute-done((bf16[1,2,128,1024]{3,2,1,0:T(8,128)(2,1)S(1)}, bf16[1,2,128,1024]{3,2,1,0:T(8,128)(2,1)S(1)}, u32[]{:S(2)}, u32[]{:S(2)}) %collective-permute-start.43) | collective-permute-done | bytes 524320 | tf_op jit(solution)/shard_map/ppermute | solution.py:249
  473.4 4.4 shard_map.289
  (579 shorter events, 274.0 us)
Async XLA Ops:
  3.5 37.1 %collective-permute-start.1 = (bf16[256,3072]{1,0:T(8,128)(2,1)}, bf16[256,3072]{1,0:T(8,128)(2,1)}, u32[]{:S(2)}, u32[]{:S(2)}) collective-permute-start(bf16[256,3072]{1,0:T(8,128)(2,1)} %pad_maximum_fusion.2), channel_id=1, source_target_pairs={{0,16},{16,0},{1,17},{17,1},{2,18},{18,2},{3,19},{19,3},{4,20},{20... | collective-permute-start | bytes 4718600 | tf_op jit(solution)/shard_map/ppermute | solution.py:256
  7.5 33.1 %collective-permute-start = (bf16[13696]{0:T(1024)(128)(2,1)S(1)}, bf16[13696]{0:T(1024)(128)(2,1)S(1)}, u32[]{:S(2)}, u32[]{:S(2)}) collective-permute-start(bf16[13696]{0:T(1024)(128)(2,1)S(1)} %dynamic-update-slice.13), channel_id=1, source_target_pairs={{0,16},{16,0},{1,17},{17,1},{2,18},{18,2},{3,19},{19,3},{4,20},{20... | collective-permute-start | bytes 82184 | tf_op jit(solution)/shard_map/ppermute | solution.py:256
  44.8 23.7 %collective-permute-start.3 = (bf16[480,1024]{1,0:T(8,128)(2,1)}, bf16[480,1024]{1,0:T(8,128)(2,1)}, u32[]{:S(2)}, u32[]{:S(2)}) collective-permute-start(bf16[480,1024]{1,0:T(8,128)(2,1)} %pad_maximum_fusion.8), channel_id=1, source_target_pairs={{0,16},{16,0},{1,17},{17,1},{2,18},{18,2},{3,19},{19,3},{4,20},{20... | collective-permute-start | bytes 2949128 | tf_op jit(solution)/shard_map/ppermute | solution.py:256
  68.5 29.5 %collective-permute-start.4 = (bf16[480,1024]{1,0:T(8,128)(2,1)}, bf16[480,1024]{1,0:T(8,128)(2,1)}, u32[]{:S(2)}, u32[]{:S(2)}) collective-permute-start(bf16[480,1024]{1,0:T(8,128)(2,1)} %collective-permute-done.3), channel_id=1, source_target_pairs={{0,2},{1,3},{2,0},{3,1},{4,6},{5,7},{6,4},{7,5},{8,10},{9,11},{10,... | collective-permute-start | bytes 2949128 | tf_op jit(solution)/shard_map/ppermute | solution.py:257
  72.0 39.6 %all-to-all-start = ((bf16[16,272,128]{2,1,0:T(8,128)(2,1)}), bf16[16,272,128]{2,1,0:T(8,128)(2,1)S(1)}, u32[]{:S(2)}, u32[]{:S(2)}) async-start(bf16[16,272,128]{2,1,0:T(8,128)(2,1)} %bitcast.1), calls=%async_computation | async-start | bytes 2228224 | tf_op jit(solution)/shard_map/all_to_all | solution.py:559
  78.8 29.0 %collective-permute-start.6 = (bf16[128,2816]{1,0:T(8,128)(2,1)}, bf16[128,2816]{1,0:T(8,128)(2,1)}, u32[]{:S(2)}, u32[]{:S(2)}) collective-permute-start(bf16[128,2816]{1,0:T(8,128)(2,1)} %constant_dynamic-slice_fusion.29), channel_id=1, source_target_pairs={{0,16},{16,0},{1,17},{17,1},{2,18},{18,2},{3,19},{19,3},{4,20},{20... | collective-permute-start | bytes 2162696 | tf_op jit(solution)/shard_map/ppermute | solution.py:256
  101.8 40.4 %collective-permute-start.5 = (bf16[960,1024]{1,0:T(8,128)(2,1)}, bf16[960,1024]{1,0:T(8,128)(2,1)}, u32[]{:S(2)}, u32[]{:S(2)}) collective-permute-start(bf16[960,1024]{1,0:T(8,128)(2,1)} %pad_maximum_fusion.1), channel_id=1, source_target_pairs={{0,1},{1,0},{2,3},{3,2},{4,5},{5,4},{6,7},{7,6},{8,9},{9,8},{10,11... | collective-permute-start | bytes 5898248 | tf_op jit(solution)/shard_map/ppermute | solution.py:257
  107.8 33.6 %collective-permute-start.9 = (bf16[256,2816]{1,0:T(8,128)(2,1)}, bf16[256,2816]{1,0:T(8,128)(2,1)}, u32[]{:S(2)}, u32[]{:S(2)}) collective-permute-start(bf16[256,2816]{1,0:T(8,128)(2,1)} %constant_dynamic-slice_fusion.28), channel_id=1, source_target_pairs={{0,16},{16,0},{1,17},{17,1},{2,18},{18,2},{3,19},{19,3},{4,20},{20... | collective-permute-start | bytes 4325384 | tf_op jit(solution)/shard_map/ppermute | solution.py:256
  110.3 64.7 %collective-permute-start.12 = (bf16[256,1536]{1,0:T(8,128)(2,1)}, bf16[256,1536]{1,0:T(8,128)(2,1)}, u32[]{:S(2)}, u32[]{:S(2)}) collective-permute-start(bf16[256,1536]{1,0:T(8,128)(2,1)} %pad_maximum_fusion.9), channel_id=1, source_target_pairs={{0,1},{1,0},{2,3},{3,2},{4,5},{5,4},{6,7},{7,6},{8,9},{9,8},{10,11... | collective-permute-start | bytes 2359304 | tf_op jit(solution)/shard_map/ppermute | solution.py:257
  112.9 34.4 %all-to-all-start.1 = ((bf16[16,256,128]{2,1,0:T(8,128)(2,1)}), bf16[16,256,128]{2,1,0:T(8,128)(2,1)S(1)}, u32[]{:S(2)}, u32[]{:S(2)}) async-start(bf16[16,256,128]{2,1,0:T(8,128)(2,1)} %shard_map.280), calls=%async_computation.1 | async-start | bytes 2097152 | tf_op jit(solution)/shard_map/all_to_all | solution.py:564
  178.1 28.5 %collective-permute-start.16 = (bf16[256,1024]{1,0:T(8,128)(2,1)}, bf16[256,1024]{1,0:T(8,128)(2,1)}, u32[]{:S(2)}, u32[]{:S(2)}) collective-permute-start(bf16[256,1024]{1,0:T(8,128)(2,1)} %copy-done.37), channel_id=1, source_target_pairs={{0,1},{1,0},{2,3},{3,2},{4,5},{5,4},{6,7},{7,6},{8,9},{9,8},{10,11... | collective-permute-start | bytes 1572872 | tf_op jit(solution)/shard_map/ppermute | solution.py:257
  197.1 26.0 %collective-permute-start.13 = (bf16[1,2,2,352,512]{4,3,2,1,0:T(8,128)(2,1)}, bf16[1,2,2,352,512]{4,3,2,1,0:T(8,128)(2,1)}, u32[]{:S(2)}, u32[]{:S(2)}) collective-permute-start(bf16[1,2,2,352,512]{4,3,2,1,0:T(8,128)(2,1)} %bitcast_select_fusion.6), channel_id=1, source_target_pairs={{0,16},{1,3},{2,18},{3,1},{4,20},{5,7},{6,22},{7,5},{8,24},{9,11},... | collective-permute-start | bytes 4325384 | tf_op jit(solution)/shard_map/ppermute | solution.py:249
  198.4 28.8 %all-to-all-start.2 = ((bf16[16,256,128]{2,1,0:T(8,128)(2,1)}), bf16[16,256,128]{2,1,0:T(8,128)(2,1)S(1)}, u32[]{:S(2)}, u32[]{:S(2)}) async-start(bf16[16,256,128]{2,1,0:T(8,128)(2,1)} %bitcast.264), calls=%async_computation.2 | async-start | bytes 2097152 | tf_op jit(solution)/shard_map/all_to_all | solution.py:559
  213.4 27.9 %collective-permute-start.18 = (bf16[1,2,2,128,1408]{4,3,1,2,0:T(8,128)(2,1)}, bf16[1,2,2,128,1408]{4,3,1,2,0:T(8,128)(2,1)}, u32[]{:S(2)}, u32[]{:S(2)}) collective-permute-start(bf16[1,2,2,128,1408]{4,3,1,2,0:T(8,128)(2,1)} %bitcast_select_fusion.3), channel_id=1, source_target_pairs={{0,16},{1,5},{2,18},{3,7},{4,20},{5,1},{6,22},{7,3},{8,24},{9,13},... | collective-permute-start | bytes 4325384 | tf_op jit(solution)/shard_map/ppermute | solution.py:249
  228.5 37.3 %all-to-all-start.3 = ((bf16[16,256,128]{2,1,0:T(8,128)(2,1)}), bf16[16,256,128]{2,1,0:T(8,128)(2,1)}, u32[]{:S(2)}, u32[]{:S(2)}) async-start(bf16[16,256,128]{2,1,0:T(8,128)(2,1)} %copy-done.6), calls=%async_computation.3 | async-start | bytes 2097152 | tf_op jit(solution)/shard_map/all_to_all | solution.py:564
  239.9 47.2 %collective-permute-start.22 = (bf16[2,2,2,128,512]{4,3,2,1,0:T(8,128)(2,1)}, bf16[2,2,2,128,512]{4,3,2,1,0:T(8,128)(2,1)}, u32[]{:S(2)}, u32[]{:S(2)}) collective-permute-start(bf16[2,2,2,128,512]{4,3,2,1,0:T(8,128)(2,1)} %bitcast_select_fusion.12), channel_id=1, source_target_pairs={{0,16},{1,3},{2,18},{3,1},{4,20},{5,7},{6,22},{7,5},{8,24},{9,11},... | collective-permute-start | bytes 3145736 | tf_op jit(solution)/shard_map/ppermute | solution.py:249
  246.5 46.7 %collective-permute-start.20 = (bf16[1,2,2,128,1408]{4,3,2,1,0:T(8,128)(2,1)}, bf16[1,2,2,128,1408]{4,3,2,1,0:T(8,128)(2,1)}, u32[]{:S(2)}, u32[]{:S(2)}) collective-permute-start(bf16[1,2,2,128,1408]{4,3,2,1,0:T(8,128)(2,1)} %dynamic-slice_bitcast_fusion), channel_id=1, source_target_pairs={{0,16},{16,0},{1,17},{17,1},{2,18},{18,2},{3,19},{19,3},{4,20},{20... | collective-permute-start | bytes 4325384 | tf_op jit(solution)/shard_map/ppermute | solution.py:256
  306.8 42.0 %collective-permute-start.27 = (bf16[1,2,2,128,1024]{4,3,1,2,0:T(8,128)(2,1)}, bf16[1,2,2,128,1024]{4,3,1,2,0:T(8,128)(2,1)}, u32[]{:S(2)}, u32[]{:S(2)}) collective-permute-start(bf16[1,2,2,128,1024]{4,3,1,2,0:T(8,128)(2,1)} %bitcast_select_fusion.11), channel_id=1, source_target_pairs={{0,16},{1,5},{2,18},{3,7},{4,20},{5,1},{6,22},{7,3},{8,24},{9,13},... | collective-permute-start | bytes 3145736 | tf_op jit(solution)/shard_map/ppermute | solution.py:249
  308.9 34.7 %collective-permute-start.21 = (bf16[1,2,128,1408]{3,2,1,0:T(8,128)(2,1)}, bf16[1,2,128,1408]{3,2,1,0:T(8,128)(2,1)}, u32[]{:S(2)}, u32[]{:S(2)}) collective-permute-start(bf16[1,2,128,1408]{3,2,1,0:T(8,128)(2,1)} %bitcast_select_fusion.14), channel_id=1, source_target_pairs={{0,2},{1,5},{2,0},{3,7},{4,6},{5,1},{6,4},{7,3},{8,10},{9,13},{10,... | collective-permute-start | bytes 2162696 | tf_op jit(solution)/shard_map/ppermute | solution.py:249
  316.2 35.4 %collective-permute-start.26 = (bf16[1,128,1408]{2,1,0:T(8,128)(2,1)}, bf16[1,128,1408]{2,1,0:T(8,128)(2,1)S(1)}, u32[]{:S(2)}, u32[]{:S(2)}) collective-permute-start(bf16[1,128,1408]{2,1,0:T(8,128)(2,1)} %dynamic-slice_bitcast_fusion.4), channel_id=1, source_target_pairs={{0,2},{1,17},{2,0},{3,19},{4,6},{5,21},{6,4},{7,23},{8,10},{9,25},... | collective-permute-start | bytes 1081352 | tf_op jit(solution)/shard_map/ppermute | solution.py:249
  316.9 36.9 %collective-permute-start.29 = (bf16[1,352,512]{2,1,0:T(8,128)(2,1)}, bf16[1,352,512]{2,1,0:T(8,128)(2,1)}, u32[]{:S(2)}, u32[]{:S(2)}) collective-permute-start(bf16[1,352,512]{2,1,0:T(8,128)(2,1)} %fusion.41), channel_id=1, source_target_pairs={{0,8},{1,9},{2,10},{3,11},{4,12},{5,13},{6,14},{7,15},{8,0},{9,1},... | collective-permute-start | bytes 1081352 | tf_op jit(solution)/shard_map/ppermute | solution.py:257
  376.9 32.2 %collective-permute-start.34 = (bf16[1,128,1408]{2,1,0:T(8,128)(2,1)}, bf16[1,128,1408]{2,1,0:T(8,128)(2,1)}, u32[]{:S(2)}, u32[]{:S(2)}) collective-permute-start(bf16[1,128,1408]{2,1,0:T(8,128)(2,1)} %get-tuple-element.194), channel_id=1, source_target_pairs={{0,4},{1,3},{2,6},{3,1},{4,0},{5,7},{6,2},{7,5},{8,12},{9,11},{10,... | collective-permute-start | bytes 1081352 | tf_op jit(solution)/shard_map/ppermute | solution.py:249
  381.1 32.2 %collective-permute-start.42 = (bf16[2,128,512]{2,1,0:T(8,128)(2,1)S(1)}, bf16[2,128,512]{2,1,0:T(8,128)(2,1)}, u32[]{:S(2)}, u32[]{:S(2)}) collective-permute-start(bf16[2,128,512]{2,1,0:T(8,128)(2,1)S(1)} %fusion.54), channel_id=1, source_target_pairs={{0,8},{1,9},{2,10},{3,11},{4,12},{5,13},{6,14},{7,15},{8,0},{9,1},... | collective-permute-start | bytes 786440 | tf_op jit(solution)/shard_map/ppermute | solution.py:257
  395.1 28.6 %collective-permute-start.39 = (bf16[1,128,1408]{2,1,0:T(8,128)(2,1)}, bf16[1,128,1408]{2,1,0:T(8,128)(2,1)}, u32[]{:S(2)}, u32[]{:S(2)}) collective-permute-start(bf16[1,128,1408]{2,1,0:T(8,128)(2,1)} %get-tuple-element.207), channel_id=1, source_target_pairs={{0,4},{1,3},{2,6},{3,1},{4,0},{5,7},{6,2},{7,5},{8,12},{9,11},{10,... | collective-permute-start | bytes 1081352 | tf_op jit(solution)/shard_map/ppermute | solution.py:249
  (160 other events, 1192.8 us)
